TPU v7x, 32 devices: a whole 2x2x4 slice. The times are simulated.
32 devices in a mesh: dp: 8 (over y, x, core), pencil: 4 (over z).
Axes of the slice: x: 2, y: 2, z: 4, core: 2. Of those that a mesh axis runs over, the one named last changes fastest.
Arguments:
- jacobian: bfloat16 [8, 8, 24, 1024], P(None, 'pencil', None, 'dp'), may hold values from -0.15625 to 0.15625
- band_offsets: int32 [3, 3], replicated, may hold values from 1 to 4
- band_masks: int32 [3, 3, 4], replicated, may hold values 0 or 1
- band_weights: float32 [3, 3], replicated, may hold values from 0.2 to 0.6
Outputs:
- gram: float32 [1024, 1024], P('dp', 'pencil')
All inputs are finite; a program needn't handle non-finite values.
Results may differ from a plain program's by a relative error of at most 0.0047.
Values may be sent and summed in bfloat16 or wider, within the bound.
No kernel may reach another device: no remote copies, remote signals or barrier semaphores. Data moves between devices by JAX's collectives and lax.ppermute only.
A program may use at most 64 MiB of HBM per device.

v0:
```python
import jax
import jax.numpy as jnp
from jax import lax
from jax.sharding import PartitionSpec as P

BANDS = 3
BLOCKS = 4


def smoother(length, offsets_row, masks_row, weights_row):
    row_index = lax.broadcasted_iota(jnp.int32, (length, length), 0)
    col_index = lax.broadcasted_iota(jnp.int32, (length, length), 1)
    block_of_row = row_index // (length // BLOCKS)
    matrix = jnp.where(row_index == col_index, jnp.float32(1.0), jnp.float32(0.0))
    for which_band in range(BANDS):
        active = jnp.zeros((length, length), jnp.float32)
        for which_block in range(BLOCKS):
            active = active + jnp.where(
                block_of_row == which_block,
                masks_row[which_band, which_block].astype(jnp.float32),
                jnp.float32(0.0),
            )
        band_reach = offsets_row[which_band]
        placed = (col_index == row_index + band_reach) | (col_index == row_index - band_reach)
        matrix = matrix + jnp.where(placed, active * weights_row[which_band], jnp.float32(0.0))
    return matrix.astype(jnp.bfloat16)


def shards(jacobian, band_offsets, band_masks, band_weights):
    length_x = jacobian.shape[0]
    depth = jacobian.shape[2]
    rows_here = jacobian.shape[3]
    length_y = jacobian.shape[1] * lax.axis_size("pencil")
    smooth_x = smoother(length_x, band_offsets[0], band_masks[0], band_weights[0])
    smooth_y = smoother(length_y, band_offsets[1], band_masks[1], band_weights[1])
    smooth_z = smoother(depth, band_offsets[2], band_masks[2], band_weights[2])
    along_x = jnp.einsum(
        "ax,xyzr->ayzr", smooth_x, jacobian, preferred_element_type=jnp.float32
    ).astype(jnp.bfloat16)
    turned = lax.all_to_all(along_x, "pencil", split_axis=0, concat_axis=1, tiled=True)
    along_y = jnp.einsum(
        "by,xyzr->xbzr", smooth_y, turned, preferred_element_type=jnp.float32
    ).astype(jnp.bfloat16)
    panel = jnp.einsum(
        "cz,xyzr->xycr", smooth_z, along_y, preferred_element_type=jnp.float32
    ).astype(jnp.bfloat16)
    mine = panel.reshape(-1, rows_here)
    arrived = lax.all_gather(panel, "dp", axis=3, tiled=True)
    columns = arrived.reshape(-1, arrived.shape[3])
    fresh = lax.dot_general(
        mine, columns, (((0,), (0,)), ((), ())), preferred_element_type=jnp.float32
    )
    return lax.psum_scatter(fresh, "pencil", scatter_dimension=1, tiled=True)


def solution(mesh):
    in_specs = (P(None, "pencil", None, "dp"), P(), P(), P())
    out_specs = P("dp", "pencil")
    return jax.shard_map(shards, mesh=mesh, in_specs=in_specs, out_specs=out_specs, check_vma=False)
```

profile of v0, /device:TPU:0, one launch (start us, length us, event | category | flops | bytes accessed | tf_op | source)
XLA Modules:
  0.0 93.0 jit_solution(17363279468761457509)
XLA Ops:
  6.5 0.0 copy-start
  6.6 0.7 copy-done.1
  7.3 0.7 fusion.219
  7.9 0.6 iota_subtract_fusion.6
  8.6 0.6 iota_subtract_fusion.7
  9.2 0.0 copy-start.2
  9.2 0.0 copy-start.3
  9.2 0.6 iota_subtract_fusion.8
  9.9 0.0 copy-done.2
  9.9 0.7 fusion.221
  10.6 0.0 copy-done.3
  10.6 0.7 fusion.223
  18.6 0.0 copy-done
  18.6 2.1 %convolution_convert_fusion.2 = bf16[8,2,24,128]{3,0,2,1:T(8,128)(2,1)S(1)} fusion(bf16[8,2,24,128]{3,2,1,0:T(8,128)(2,1)S(1)} %copy-done, f32[]{:T(128)} %bitcast.18, f32[]{:T(128)} %bitcast.17, f32[]{:T(128)} %bitcast.16, f32[]{:T(128)} %bitcast.15, f32[]{:T(128)} %bitcast.14, s32[8]{0:T(128)S(1)} %get-tuple-element.62, s32[8]{0:T(128)S(1)} %get-tuple-element.63, ...), kind=kOutput, calls=%fused_computation.3 | convolution fusion | flops 838592 | bytes 196932 | tf_op jit(solution)/shard_map/ax,xyzr->ayzr/dot_general | solution.py:37
  20.7 0.7 copy.13
  21.3 6.3 %all-to-all-start = ((bf16[8,2,24,128]{3,2,1,0:T(8,128)(2,1)}), bf16[8,2,24,128]{3,2,1,0:T(8,128)(2,1)S(1)}, u32[]{:S(2)}, u32[]{:S(2)}) async-start(bf16[8,2,24,128]{3,2,1,0:T(8,128)(2,1)} %copy.13), calls=%async_computation | async-start | bytes 196608 | tf_op jit(solution)/shard_map/all_to_all | solution.py:40
  27.7 0.0 reduce-scatter.2.cloned.1.call-start
  27.7 0.6 iota_subtract_fusion.2
  28.3 0.7 iota_subtract_fusion.3
  29.0 0.6 iota_subtract_fusion.4
  29.6 0.6 iota_subtract_fusion.5
  30.2 0.6 iota_subtract_fusion
  30.8 0.7 fusion.220
  31.5 0.7 fusion.222
  47.0 0.6 iota_subtract_fusion.1
  47.6 0.0 all-to-all-done
  47.6 2.2 %fusion = bf16[2,8,24,128]{3,1,2,0:T(8,128)(2,1)S(1)} fusion(bf16[2,8,24,128]{3,2,1,0:T(8,128)(2,1)S(1)} %bitcast.90, f32[]{:T(128)} %bitcast.42, f32[]{:T(128)} %bitcast.41, f32[]{:T(128)} %bitcast.40, f32[]{:T(128)} %bitcast.39, f32[]{:T(128)} %bitcast.38, s32[8]{0:T(128)S(1)} %get-tuple-element.70, s32[8]{0:T(128)S(1)} %get-tuple-element.71, ...), kind=kOutput, calls=%fused_computation.4 | convolution fusion | flops 838592 | bytes 196932 | tf_op jit(solution)/shard_map/by,xyzr->xbzr/dot_general | solution.py:41
  49.9 2.2 %fusion.1 = bf16[2,8,24,128]{3,2,1,0:T(8,128)(2,1)S(1)} fusion(bf16[2,8,24,128]{3,1,2,0:T(8,128)(2,1)S(1)} %fusion, f32[]{:T(128)} %bitcast.64, f32[]{:T(128)} %bitcast.63, f32[]{:T(128)} %bitcast.62, f32[]{:T(128)} %bitcast.61, f32[]{:T(128)} %bitcast.60, s32[24]{0:T(128)S(1)} %get-tuple-element.76, s32[24]{0:T(128)S(1)} %get-tuple-element.77, ...), kind=kOutput, calls=%fused_computation.5 | convolution fusion | flops 2435520 | bytes 197460 | tf_op jit(solution)/shard_map/cz,xyzr->xycr/dot_general | solution.py:44
  52.0 10.6 %all_gather.3 = bf16[2,8,24,1024]{3,2,1,0:T(8,128)(2,1)S(1)} all-gather(bf16[2,8,24,128]{3,2,1,0:T(8,128)(2,1)S(1)} %fusion.1), channel_id=1, replica_groups=mesh['dp'=8,'pencil'=4] {'dp'}, dimensions={3}, use_global_device_ids=true | all-gather | bytes 884736 | tf_op jit(solution)/shard_map/all_gather | solution.py:48
  62.6 1.1 %convolution_bitcast_fusion = f32[128,1024]{1,0:T(8,128)} fusion(bf16[2,8,24,128]{3,2,1,0:T(8,128)(2,1)S(1)} %fusion.1, bf16[2,8,24,1024]{3,2,1,0:T(8,128)(2,1)S(1)} %all_gather.3), kind=kOutput, calls=%fused_computation | convolution fusion | flops 100663296 | bytes 1409024 | tf_op jit(solution)/shard_map/dot_general | solution.py:50
  63.8 0.0 reduce-scatter.2.cloned.1.call-update
  63.8 22.3 %reduce-scatter.2.cloned.1.call-done = f32[128,256]{1,0:T(8,128)} async-done(((f32[128,1024]{1,0:T(8,128)}), f32[128,256]{1,0:T(8,128)}) %reduce-scatter.2.cloned.1.call-update) | async-done | bytes 131088 | tf_op jit(solution)/shard_map/reduce_scatter | solution.py:53
  (7 shorter events, 0.0 us)
Async XLA Ops:
  6.5 12.0 %copy-start = (bf16[8,2,24,128]{3,2,1,0:T(8,128)(2,1)S(1)}, bf16[8,2,24,128]{3,2,1,0:T(8,128)(2,1)}, u32[]{:S(2)}) copy-start(bf16[8,2,24,128]{3,2,1,0:T(8,128)(2,1)} %param.4) | copy-start | bytes 294916
  6.5 0.7 copy-start.1
  9.2 0.7 copy-start.2
  9.2 1.4 %copy-start.3 = (s32[3,3,4]{2,1,0:T(4,128)S(1)}, s32[3,3,4]{2,1,0:T(4,128)}, u32[]{:S(2)}) copy-start(s32[3,3,4]{2,1,0:T(4,128)} %param.6) | copy-start | bytes 436
  21.3 26.3 %all-to-all-start = ((bf16[8,2,24,128]{3,2,1,0:T(8,128)(2,1)}), bf16[8,2,24,128]{3,2,1,0:T(8,128)(2,1)S(1)}, u32[]{:S(2)}, u32[]{:S(2)}) async-start(bf16[8,2,24,128]{3,2,1,0:T(8,128)(2,1)} %copy.13), calls=%async_computation | async-start | bytes 196608 | tf_op jit(solution)/shard_map/all_to_all | solution.py:40
  27.7 58.5 %reduce-scatter.2.cloned.1.call-start = ((), (), s32[]{:S(2)}) async-start(), calls=%async_computation.2 | async-start | bytes 655360 | tf_op jit(solution)/shard_map/reduce_scatter | solution.py:53
Sparse Core Ops, SparseCore 0:
  63.9 22.1 reduce-scatter.1
where the time goes:
time: 93.7 us; the launch traced here: 93 us
  between operations  35.6 us (38%)
  waiting for transfers between devices  22.4 us (24%)
  blocking collectives  10.6 us (11%)
  matrix products  7.63 us (8%)
  starting transfers between devices  6.32 us (7%)
  other arithmetic  5.63 us (6%)
  local copies, waits for them, and re-layouts  4.82 us (5%)
    reduce_scatter x1, waiting for transfers between devices, shards(): return lax.psum_scatter(fresh, 'pencil', scatter_dimension=1, tiled=True)  22.3 us
    all_gather x1, blocking collectives, shards(): arrived = lax.all_gather(panel, 'dp', axis=3, tiled=True)  10.6 us
    all_to_all x1, starting transfers between devices, shards(): lax.all_to_all(along_x, 'pencil', split_axis=0, concat_axis=1, tiled=True)  6.32 us
    sub x9, other arithmetic, smoother(): row_index - band_reach  5.6 us
    dot_general x1, matrix products, shards(): jnp.einsum('by,xyzr->xbzr', smooth_y, turned, preferred_element_type=jnp....  2.22 us
    dot_general x1, matrix products, shards(): jnp.einsum('cz,xyzr->xycr', smooth_z, along_y, preferred_element_type=jnp...  2.18 us
    dot_general x1, matrix products, shards(): jnp.einsum('ax,xyzr->ayzr', smooth_x, jacobian, preferred_element_type=jn...  2.1 us
    slice x3, local copies, waits for them, and re-layouts, smoother(): masks_row[which_band, which_block].astype(jnp.float32)  2.06 us
  transfers between devices with their start and end apart: 2, of which 1 were waited for; matrix products, arithmetic and copies ran while one was open for 5% of the time, Pallas kernels for 0%

commit v1 on v0

v1 whole, which is shorter than its diff:
```python
import functools

import jax
import jax.numpy as jnp
from jax import lax
from jax.experimental import pallas as pl
from jax.experimental.pallas import tpu as pltpu
from jax.sharding import PartitionSpec as P

BANDS = 3
BLOCKS = 4
LANES = 128
CORES = 2
COLUMNS_AT_ONCE = 8
VMEM = pl.BlockSpec(memory_space=pltpu.VMEM)
SMEM = pl.BlockSpec(memory_space=pltpu.SMEM)


def farthest(rank, plane, planes):
    mirrored = planes - 1 - plane
    if isinstance(plane, int) and isinstance(rank, int):
        alone, reach, outer = abs(plane - mirrored), min(plane, mirrored), rank if plane > mirrored else planes - 1 - rank
        pair = rank - alone
        inner = plane - (reach - pair // 2) if pair % 2 == 0 else plane + (reach - pair // 2)
        return outer if rank < alone else inner
    alone, reach = jnp.abs(plane - mirrored), jnp.minimum(plane, mirrored)
    outer = jnp.where(plane > mirrored, rank, planes - 1 - rank)
    pair = rank - alone
    away = reach - (pair >> 1)
    inner = jnp.where((pair & 1) == 0, plane - away, plane + away)
    return jnp.where(rank < alone, outer, inner)


def smoother(distance, owner, axis, length, offsets, masks, weights):
    matrix = jnp.where(distance == 0, jnp.float32(1.0), jnp.float32(0.0))
    for band in range(BANDS):
        value = masks[axis, band, 0].astype(jnp.float32) * weights[axis, band]
        for block in range(1, BLOCKS):
            here = masks[axis, band, block].astype(jnp.float32) * weights[axis, band]
            value = jnp.where(owner >= block * (length // BLOCKS), here, value)
        matrix = matrix + jnp.where(distance == offsets[axis, band], value, jnp.float32(0.0))
    return matrix.astype(jnp.bfloat16)


def write_gram(table, axis, length, params):
    row = lax.broadcasted_iota(jnp.int32, (LANES, LANES), 0)
    col = lax.broadcasted_iota(jnp.int32, (LANES, LANES), 1)
    distance = jnp.where((row < length) & (col < length), jnp.abs(row - col), -1)
    gram = jnp.dot(
        smoother(distance, col, axis, length, *params),
        smoother(distance, row, axis, length, *params),
        preferred_element_type=jnp.float32,
    )
    for place in range(length):
        table[place] = jnp.broadcast_to(gram[:length, place : place + 1], (length, LANES))


def mix_x_z_kernel(dims, offsets, masks, weights, field, out, along_z, table):
    length_x, width, depth = dims
    params = (offsets, masks, weights)
    write_gram(table, 0, length_x, params)
    rows = COLUMNS_AT_ONCE * depth
    shape = (COLUMNS_AT_ONCE, depth, rows)
    row_z = lax.broadcasted_iota(jnp.int32, shape, 1)
    row_group = lax.broadcasted_iota(jnp.int32, shape, 0)
    lane = lax.broadcasted_iota(jnp.int32, shape, 2)
    lane_group = jnp.zeros(shape, jnp.int32)
    for group in range(1, COLUMNS_AT_ONCE):
        lane_group = lane_group + jnp.where(lane >= group * depth, 1, 0)
    lane_z = lane - lane_group * depth
    distance = jnp.where(row_group == lane_group, jnp.abs(row_z - lane_z), -1)
    forth = smoother(distance, row_z, 2, depth, *params).astype(jnp.float32).reshape(rows, rows).astype(jnp.bfloat16)
    back = smoother(distance, lane_z, 2, depth, *params).astype(jnp.float32).reshape(rows, rows).astype(jnp.bfloat16)
    pieces = length_x * width // COLUMNS_AT_ONCE
    for first in range(0, pieces, 2):
        held = jnp.concatenate([field[piece * rows : (piece + 1) * rows, :] for piece in (first, first + 1)], axis=1)
        once = jnp.dot(forth, held, preferred_element_type=jnp.float32)
        high = once.astype(jnp.bfloat16)
        low = (once - high.astype(jnp.float32)).astype(jnp.bfloat16)
        twice = jnp.dot(back, high, preferred_element_type=jnp.float32) + jnp.dot(back, low, preferred_element_type=jnp.float32)
        for piece in (0, 1):
            along_z[(first + piece) * rows : (first + piece + 1) * rows, :] = twice[:, piece * LANES : (piece + 1) * LANES]
    slab = width * depth

    def one_x(x):
        total = table[0, pl.ds(x, 1), :] * along_z[0:slab, :]
        for other in range(1, length_x):
            total = total + table[other, pl.ds(x, 1), :] * along_z[other * slab : (other + 1) * slab, :]
        start = pl.multiple_of(x * slab, 16)
        out[pl.ds(start, slab), :] = total.astype(jnp.bfloat16)

    if length_x <= 8:
        for x in range(length_x):
            one_x(x)
    else:
        pl.loop(0, length_x)(one_x)


def mix_y_kernel(dims, planes, offsets, masks, weights, *refs):
    length_x, width, depth = dims
    blocks, (out, fields, mixed, table) = refs[:planes], refs[planes:]
    length_y = planes * width
    cells = length_x * width * depth
    write_gram(table, 1, length_y, (offsets, masks, weights))
    plane = lax.axis_index("pencil")
    chip = lax.axis_index("dp") >> 1
    for away in range(planes):
        wide = blocks[away][...].astype(jnp.float32).reshape(length_x, width, depth, LANES)
        for y in range(width):
            fields[(plane ^ away) * width + y] = wide[:, y]

    def one_x(x, place, y):
        total = table[0, pl.ds(place, 1), :] * fields[0, x]
        for other in range(1, length_y):
            total = total + table[other, pl.ds(place, 1), :] * fields[other, x]
        start = (x * width + y) * depth
        mixed[pl.ds(start if isinstance(start, int) else pl.multiple_of(start, 8), depth), :] = total

    for away in range(planes):
        slab = farthest((chip ^ away) ^ plane, plane, planes)
        for y in range(width):
            place = slab * width + y
            if length_x <= 8:
                for x in range(length_x):
                    one_x(x, place, y)
            else:
                pl.loop(0, length_x)(functools.partial(one_x, place=place, y=y))
        for first in range(0, cells, LANES):
            out[away, :, first : first + LANES] = mixed[first : first + LANES, :].T.astype(jnp.bfloat16)


def gram_kernel(planes, mixed, *refs):
    mine, theirs, out = refs[:planes], refs[planes : 2 * planes], refs[2 * planes]
    total = None
    for away in range(planes):
        both = jnp.concatenate([mine[away][...], theirs[away][...]], axis=1)
        part = jnp.dot(mixed[away], both, preferred_element_type=jnp.float32)
        total = part if total is None else total + part
    core = lax.axis_index("dp") & 1
    out[:, pl.ds(pl.multiple_of(core * LANES, LANES), LANES)] = total[:, :LANES]
    out[:, pl.ds(pl.multiple_of((1 - core) * LANES, LANES), LANES)] = total[:, LANES:]


def call(kernel, out_shape, operands, in_specs, scratch=(), flops=0):
    sizes = [out_shape] + list(operands)
    held = sum(item.size * item.dtype.itemsize for item in sizes)
    spare = sum(4 * int(functools.reduce(lambda a, b: a * b, item.shape)) for item in scratch)
    return pl.pallas_call(
        kernel,
        out_shape=out_shape,
        in_specs=in_specs,
        out_specs=VMEM,
        scratch_shapes=list(scratch),
        compiler_params=pltpu.CompilerParams(vmem_limit_bytes=(6 << 20) + 2 * held + spare),
        cost_estimate=pl.CostEstimate(flops=flops, bytes_accessed=held, transcendentals=0),
    )(*operands)


def shards(jacobian, band_offsets, band_masks, band_weights):
    length_x, width, depth, rows = jacobian.shape
    planes, spread = lax.axis_size("pencil"), lax.axis_size("dp")
    dims = (length_x, width, depth)
    cells = length_x * width * depth
    params = (band_offsets, band_masks, band_weights)
    field = jacobian.reshape(cells, rows)

    route = []
    for source in range(spread):
        for plane in range(planes):
            target_plane = source // CORES
            rank = [farthest(r, target_plane, planes) for r in range(planes)].index(plane)
            target = (target_plane ^ rank) * CORES + source % CORES
            route.append((source * planes + plane, target * planes + target_plane))
    arrived = lax.ppermute(field, ("dp", "pencil"), route)

    mixed_x_z = call(
        functools.partial(mix_x_z_kernel, dims),
        jax.ShapeDtypeStruct((cells, rows), jnp.bfloat16),
        (*params, field),
        [SMEM] * 3 + [VMEM],
        [pltpu.VMEM((cells, LANES), jnp.float32), pltpu.VMEM((length_x, length_x, LANES), jnp.float32)],
    )
    along = [mixed_x_z] + [
        lax.ppermute(mixed_x_z, "pencil", [(i, i ^ away) for i in range(planes)]) for away in range(1, planes)
    ]
    mine = [arrived] + [
        lax.ppermute(arrived, "dp", [(i, i ^ (away * CORES)) for i in range(spread)]) for away in range(1, planes)
    ]
    theirs = [lax.ppermute(block, "dp", [(i, i ^ 1) for i in range(spread)]) for block in mine]
    length_y = planes * width
    mixed = call(
        functools.partial(mix_y_kernel, dims, planes),
        jax.ShapeDtypeStruct((planes, rows, cells), jnp.bfloat16),
        (*params, *along),
        [SMEM] * 3 + [VMEM] * planes,
        [
            pltpu.VMEM((length_y, length_x, depth, LANES), jnp.float32),
            pltpu.VMEM((cells, LANES), jnp.float32),
            pltpu.VMEM((length_y, length_y, LANES), jnp.float32),
        ],
    )
    return call(
        functools.partial(gram_kernel, planes),
        jax.ShapeDtypeStruct((rows, CORES * rows), jnp.float32),
        (mixed, *mine, *theirs),
        [VMEM] * (1 + 2 * planes),
    )


def solution(mesh):
    in_specs = (P(None, "pencil", None, "dp"), P(), P(), P())
    out_specs = P("dp", "pencil")
    return jax.shard_map(shards, mesh=mesh, in_specs=in_specs, out_specs=out_specs, check_vma=False)
```

time: 93.7 us -> 23.7 us (0.25)
  the two profiles are of different devices: /device:TPU:0 before, /device:TPU:14 now
where the time goes in v1:
time: 23.7 us; the launch traced here: 23.5 us
  starting transfers between devices  10.9 us (46%)
  waiting for transfers between devices  5.89 us (25%)
  Pallas kernels  3.58 us (15%)
  local copies, waits for them, and re-layouts  2.99 us (13%)
    ppermute x3, waiting for transfers between devices, shards(): lax.ppermute(mixed_x_z, 'pencil', [(i, i ^ away) for i in range(planes)])  5.83 us
    ppermute x3, starting transfers between devices, shards(): lax.ppermute(mixed_x_z, 'pencil', [(i, i ^ away) for i in range(planes)])  3.92 us
    pallas_call x3, Pallas kernels, call(): pl.pallas_call(kernel, out_shape=out_shape, in_specs=in_specs, out_specs=...  3.58 us
    ppermute x3, starting transfers between devices, shards(): lax.ppermute(arrived, 'dp', [(i, i ^ away * CORES) for i in range(spread)])  3.49 us
    unnamed x12, local copies, waits for them, and re-layouts  2.99 us
    ppermute x1, starting transfers between devices, shards(): arrived = lax.ppermute(field, ('dp', 'pencil'), route)  2.56 us
    ppermute x4, starting transfers between devices, shards(): lax.ppermute(block, 'dp', [(i, i ^ 1) for i in range(spread)])  0.97 us
  transfers between devices with their start and end apart: 11, of which 2 were waited for; matrix products, arithmetic and copies ran while one was open for 0% of the time, Pallas kernels for 11%

profile of v1, /device:TPU:14, one launch (start us, length us, event | category | flops | bytes accessed | tf_op | source)
XLA Modules:
  0.0 23.5 jit_solution(18107349386512701949)
XLA Ops:
  0.0 2.6 %collective-permute-start.3 = (bf16[384,128]{1,0:T(8,128)(2,1)}, bf16[384,128]{1,0:T(8,128)(2,1)S(1)}, u32[]{:S(2)}, u32[]{:S(2)}) collective-permute-start(bf16[384,128]{1,0:T(8,128)(2,1)} %bitcast.1), channel_id=1, source_target_pairs={{0,24},{1,16},{2,8},{3,0},{4,28},{5,20},{6,12},{7,4},{8,1},{9,17},... | collective-permute-start | bytes 294920 | tf_op jit(solution)/shard_map/ppermute | solution.py:174
  2.6 0.0 copy-start
  2.6 0.9 %copy-done = bf16[8,2,24,128]{3,2,1,0:T(8,128)(2,1)S(1)} copy-done((bf16[8,2,24,128]{3,2,1,0:T(8,128)(2,1)S(1)}, bf16[8,2,24,128]{3,2,1,0:T(8,128)(2,1)}, u32[]{:S(2)}) %copy-start) | copy-done | bytes 98328
  3.5 0.7 %copy-done.1 = s32[3,3,4]{2,1,0:T(4,128)S(1)} copy-done((s32[3,3,4]{2,1,0:T(4,128)S(1)}, s32[3,3,4]{2,1,0:T(4,128)}, u32[]{:S(2)}) %copy-start.1) | copy-done | bytes 168
  4.2 0.7 %copy-done.3 = s32[3,3]{1,0:T(4,128)S(1)} copy-done((s32[3,3]{1,0:T(4,128)S(1)}, s32[3,3]{1,0:T(4,128)}, u32[]{:S(2)}) %copy-start.3) | copy-done | bytes 60
  4.9 0.7 %copy-done.5 = f32[3,3]{1,0:T(4,128)S(1)} copy-done((f32[3,3]{1,0:T(4,128)S(1)}, f32[3,3]{1,0:T(4,128)}, u32[]{:S(2)}) %copy-start.5) | copy-done | bytes 60
  5.5 1.2 %shard_map.46.refs_0_ = bf16[384,128]{1,0:T(8,128)(2,1)S(1)} custom-call(s32[3,3]{1,0:T(4,128)S(1)} %copy-done.3, s32[3,3,4]{2,1,0:T(4,128)S(1)} %copy-done.1, f32[3,3]{1,0:T(4,128)S(1)} %copy-done.5, bf16[384,128]{1,0:T(8,128)(2,1)S(1)} %bitcast.2), custom_call_target="tpu_custom_call" | custom-call | bytes 196824 | tf_op jit(solution)/shard_map/pallas_call | solution.py:148
  6.8 0.6 %collective-permute-start.2 = (bf16[384,128]{1,0:T(8,128)(2,1)S(1)}, bf16[384,128]{1,0:T(8,128)(2,1)S(1)}, u32[]{:S(2)}, u32[]{:S(2)}) collective-permute-start(bf16[384,128]{1,0:T(8,128)(2,1)S(1)} %shard_map.46.refs_0_), channel_id=1, source_target_pairs={{0,3},{1,2},{2,1},{3,0},{4,7},{5,6},{6,5},{7,4},{8,11},{9,10},{10,... | collective-permute-start | bytes 294920 | tf_op jit(solution)/shard_map/ppermute | solution.py:184
  7.4 3.3 %collective-permute-start.1 = (bf16[384,128]{1,0:T(8,128)(2,1)S(1)}, bf16[384,128]{1,0:T(8,128)(2,1)S(1)}, u32[]{:S(2)}, u32[]{:S(2)}) collective-permute-start(bf16[384,128]{1,0:T(8,128)(2,1)S(1)} %shard_map.46.refs_0_), channel_id=1, source_target_pairs={{0,2},{1,3},{2,0},{3,1},{4,6},{5,7},{6,4},{7,5},{8,10},{9,11},{10,... | collective-permute-start | bytes 294920 | tf_op jit(solution)/shard_map/ppermute | solution.py:184
  10.7 0.0 collective-permute-done.3.refs_0_
  10.7 0.0 collective-permute-start.6
  10.7 1.0 %collective-permute-start.5 = (bf16[384,128]{1,0:T(8,128)(2,1)S(1)}, bf16[384,128]{1,0:T(8,128)(2,1)S(1)}, u32[]{:S(2)}, u32[]{:S(2)}) collective-permute-start(bf16[384,128]{1,0:T(8,128)(2,1)S(1)} %collective-permute-done.3.refs_0_), channel_id=1, source_target_pairs={{0,16},{4,20},{8,24},{12,28},{16,0},{20,4},{24,8},{28,12},{1,17},{... | collective-permute-start | bytes 294920 | tf_op jit(solution)/shard_map/ppermute | solution.py:187
  11.7 2.5 %collective-permute-start.4 = (bf16[384,128]{1,0:T(8,128)(2,1)S(1)}, bf16[384,128]{1,0:T(8,128)(2,1)S(1)}, u32[]{:S(2)}, u32[]{:S(2)}) collective-permute-start(bf16[384,128]{1,0:T(8,128)(2,1)S(1)} %collective-permute-done.3.refs_0_), channel_id=1, source_target_pairs={{0,8},{4,12},{8,0},{12,4},{16,24},{20,28},{24,16},{28,20},{1,9},{5... | collective-permute-start | bytes 294920 | tf_op jit(solution)/shard_map/ppermute | solution.py:187
  14.2 2.2 %collective-permute-done.2.refs_3_ = bf16[384,128]{1,0:T(8,128)(2,1)S(1)} collective-permute-done((bf16[384,128]{1,0:T(8,128)(2,1)S(1)}, bf16[384,128]{1,0:T(8,128)(2,1)S(1)}, u32[]{:S(2)}, u32[]{:S(2)}) %collective-permute-start.2) | collective-permute-done | bytes 98336 | tf_op jit(solution)/shard_map/ppermute | solution.py:184
  16.4 0.0 collective-permute-start
  16.4 0.0 collective-permute-done.1.refs_2_
  16.4 0.0 collective-permute-start.7
  16.4 0.0 collective-permute-done.6.refs_3_
  16.5 0.5 %collective-permute-start.10 = (bf16[384,128]{1,0:T(8,128)(2,1)S(1)}, bf16[384,128]{1,0:T(8,128)(2,1)S(1)}, u32[]{:S(2)}, u32[]{:S(2)}) collective-permute-start(bf16[384,128]{1,0:T(8,128)(2,1)S(1)} %collective-permute-done.6.refs_3_), channel_id=1, source_target_pairs={{0,4},{4,0},{8,12},{12,8},{16,20},{20,16},{24,28},{28,24},{1,5},{5... | collective-permute-start | bytes 294920 | tf_op jit(solution)/shard_map/ppermute | solution.py:189
  16.9 0.0 collective-permute-done.5.refs_2_
  16.9 0.1 collective-permute-start.9
  17.0 0.0 collective-permute-done.4.refs_1_
  17.0 0.4 %collective-permute-start.8 = (bf16[384,128]{1,0:T(8,128)(2,1)S(1)}, bf16[384,128]{1,0:T(8,128)(2,1)S(1)}, u32[]{:S(2)}, u32[]{:S(2)}) collective-permute-start(bf16[384,128]{1,0:T(8,128)(2,1)S(1)} %collective-permute-done.4.refs_1_), channel_id=1, source_target_pairs={{0,4},{4,0},{8,12},{12,8},{16,20},{20,16},{24,28},{28,24},{1,5},{5... | collective-permute-start | bytes 294920 | tf_op jit(solution)/shard_map/ppermute | solution.py:189
  17.5 3.6 %collective-permute-done.refs_1_ = bf16[384,128]{1,0:T(8,128)(2,1)S(1)} collective-permute-done((bf16[384,128]{1,0:T(8,128)(2,1)S(1)}, bf16[384,128]{1,0:T(8,128)(2,1)S(1)}, u32[]{:S(2)}, u32[]{:S(2)}) %collective-permute-start) | collective-permute-done | bytes 98336 | tf_op jit(solution)/shard_map/ppermute | solution.py:184
  21.0 0.0 copy-done.2
  21.0 0.0 copy-done.4
  21.0 1.4 %shard_map.47.mixed = bf16[4,128,384]{2,1,0:T(8,128)(2,1)S(1)} custom-call(s32[3,3]{1,0:T(4,128)S(1)} %copy-done.4, s32[3,3,4]{2,1,0:T(4,128)S(1)} %copy-done.2, f32[3,3]{1,0:T(4,128)S(1)} %copy-done.5, bf16[384,128]{1,0:T(8,128)(2,1)S(1)} %shard_map.46.refs_0_, bf16[384,128]{1,0:T(8,128)(2,1)S(1)} %collective-permute-done.refs_1_, ...), custom_call_target="tpu_custom_call" | custom-call | bytes 786648 | tf_op jit(solution)/shard_map/pallas_call | solution.py:148
  22.5 0.0 collective-permute-done.7.refs_4_
  22.5 0.0 collective-permute-done.10.refs_7_
  22.5 0.0 collective-permute-done.9.refs_6_
  22.5 0.0 collective-permute-done.8.refs_5_
  22.5 1.0 %shard_map.48 = f32[128,256]{1,0:T(8,128)} custom-call(bf16[4,128,384]{2,1,0:T(8,128)(2,1)S(1)} %shard_map.47.mixed, bf16[384,128]{1,0:T(8,128)(2,1)S(1)} %collective-permute-done.3.refs_0_, bf16[384,128]{1,0:T(8,128)(2,1)S(1)} %collective-permute-done.4.refs_1_, bf16[384,128]{1,0:T(8,128)(2,1)S(1)} %collective-permute-done.5.refs_2_, ...), custom_call_target="tpu_custom_call" | custom-call | bytes 1310720 | tf_op jit(solution)/shard_map/pallas_call | solution.py:148
  (5 shorter events, 0.0 us)
Async XLA Ops:
  0.0 10.7 %collective-permute-start.3 = (bf16[384,128]{1,0:T(8,128)(2,1)}, bf16[384,128]{1,0:T(8,128)(2,1)S(1)}, u32[]{:S(2)}, u32[]{:S(2)}) collective-permute-start(bf16[384,128]{1,0:T(8,128)(2,1)} %bitcast.1), channel_id=1, source_target_pairs={{0,24},{1,16},{2,8},{3,0},{4,28},{5,20},{6,12},{7,4},{8,1},{9,17},... | collective-permute-start | bytes 294920 | tf_op jit(solution)/shard_map/ppermute | solution.py:174
  2.6 0.9 %copy-start = (bf16[8,2,24,128]{3,2,1,0:T(8,128)(2,1)S(1)}, bf16[8,2,24,128]{3,2,1,0:T(8,128)(2,1)}, u32[]{:S(2)}) copy-start(bf16[8,2,24,128]{3,2,1,0:T(8,128)(2,1)} %param.4) | copy-start | bytes 294916
  3.5 0.7 %copy-start.1 = (s32[3,3,4]{2,1,0:T(4,128)S(1)}, s32[3,3,4]{2,1,0:T(4,128)}, u32[]{:S(2)}) copy-start(s32[3,3,4]{2,1,0:T(4,128)} %masks.3) | copy-start | bytes 436
  4.2 0.7 %copy-start.3 = (s32[3,3]{1,0:T(4,128)S(1)}, s32[3,3]{1,0:T(4,128)}, u32[]{:S(2)}) copy-start(s32[3,3]{1,0:T(4,128)} %offsets.3) | copy-start | bytes 112
  4.9 0.7 %copy-start.5 = (f32[3,3]{1,0:T(4,128)S(1)}, f32[3,3]{1,0:T(4,128)}, u32[]{:S(2)}) copy-start(f32[3,3]{1,0:T(4,128)} %weights.3) | copy-start | bytes 112
  5.5 15.5 %copy-start.2 = (s32[3,3,4]{2,1,0:T(4,128)S(1)}, s32[3,3,4]{2,1,0:T(4,128)}, u32[]{:S(2)}) copy-start(s32[3,3,4]{2,1,0:T(4,128)} %masks.3) | copy-start | bytes 436
  5.5 15.5 %copy-start.4 = (s32[3,3]{1,0:T(4,128)S(1)}, s32[3,3]{1,0:T(4,128)}, u32[]{:S(2)}) copy-start(s32[3,3]{1,0:T(4,128)} %offsets.3) | copy-start | bytes 112
  6.8 9.7 %collective-permute-start.2 = (bf16[384,128]{1,0:T(8,128)(2,1)S(1)}, bf16[384,128]{1,0:T(8,128)(2,1)S(1)}, u32[]{:S(2)}, u32[]{:S(2)}) collective-permute-start(bf16[384,128]{1,0:T(8,128)(2,1)S(1)} %shard_map.46.refs_0_), channel_id=1, source_target_pairs={{0,3},{1,2},{2,1},{3,0},{4,7},{5,6},{6,5},{7,4},{8,11},{9,10},{10,... | collective-permute-start | bytes 294920 | tf_op jit(solution)/shard_map/ppermute | solution.py:184
  7.4 9.1 %collective-permute-start.1 = (bf16[384,128]{1,0:T(8,128)(2,1)S(1)}, bf16[384,128]{1,0:T(8,128)(2,1)S(1)}, u32[]{:S(2)}, u32[]{:S(2)}) collective-permute-start(bf16[384,128]{1,0:T(8,128)(2,1)S(1)} %shard_map.46.refs_0_), channel_id=1, source_target_pairs={{0,2},{1,3},{2,0},{3,1},{4,6},{5,7},{6,4},{7,5},{8,10},{9,11},{10,... | collective-permute-start | bytes 294920 | tf_op jit(solution)/shard_map/ppermute | solution.py:184
  10.7 5.8 %collective-permute-start.6 = (bf16[384,128]{1,0:T(8,128)(2,1)S(1)}, bf16[384,128]{1,0:T(8,128)(2,1)S(1)}, u32[]{:S(2)}, u32[]{:S(2)}) collective-permute-start(bf16[384,128]{1,0:T(8,128)(2,1)S(1)} %collective-permute-done.3.refs_0_), channel_id=1, source_target_pairs={{0,24},{4,28},{8,16},{12,20},{16,8},{20,12},{24,0},{28,4},{1,25},{... | collective-permute-start | bytes 294920 | tf_op jit(solution)/shard_map/ppermute | solution.py:187
  10.7 6.3 %collective-permute-start.5 = (bf16[384,128]{1,0:T(8,128)(2,1)S(1)}, bf16[384,128]{1,0:T(8,128)(2,1)S(1)}, u32[]{:S(2)}, u32[]{:S(2)}) collective-permute-start(bf16[384,128]{1,0:T(8,128)(2,1)S(1)} %collective-permute-done.3.refs_0_), channel_id=1, source_target_pairs={{0,16},{4,20},{8,24},{12,28},{16,0},{20,4},{24,8},{28,12},{1,17},{... | collective-permute-start | bytes 294920 | tf_op jit(solution)/shard_map/ppermute | solution.py:187
  11.7 5.4 %collective-permute-start.4 = (bf16[384,128]{1,0:T(8,128)(2,1)S(1)}, bf16[384,128]{1,0:T(8,128)(2,1)S(1)}, u32[]{:S(2)}, u32[]{:S(2)}) collective-permute-start(bf16[384,128]{1,0:T(8,128)(2,1)S(1)} %collective-permute-done.3.refs_0_), channel_id=1, source_target_pairs={{0,8},{4,12},{8,0},{12,4},{16,24},{20,28},{24,16},{28,20},{1,9},{5... | collective-permute-start | bytes 294920 | tf_op jit(solution)/shard_map/ppermute | solution.py:187
  16.4 4.6 %collective-permute-start = (bf16[384,128]{1,0:T(8,128)(2,1)S(1)}, bf16[384,128]{1,0:T(8,128)(2,1)S(1)}, u32[]{:S(2)}, u32[]{:S(2)}) collective-permute-start(bf16[384,128]{1,0:T(8,128)(2,1)S(1)} %shard_map.46.refs_0_), channel_id=1, source_target_pairs={{0,1},{1,0},{2,3},{3,2},{4,5},{5,4},{6,7},{7,6},{8,9},{9,8},{10,11... | collective-permute-start | bytes 294920 | tf_op jit(solution)/shard_map/ppermute | solution.py:184
  16.4 6.1 %collective-permute-start.7 = (bf16[384,128]{1,0:T(8,128)(2,1)S(1)}, bf16[384,128]{1,0:T(8,128)(2,1)S(1)}, u32[]{:S(2)}, u32[]{:S(2)}) collective-permute-start(bf16[384,128]{1,0:T(8,128)(2,1)S(1)} %collective-permute-done.3.refs_0_), channel_id=1, source_target_pairs={{0,4},{4,0},{8,12},{12,8},{16,20},{20,16},{24,28},{28,24},{1,5},{5... | collective-permute-start | bytes 294920 | tf_op jit(solution)/shard_map/ppermute | solution.py:189
  16.5 6.0 %collective-permute-start.10 = (bf16[384,128]{1,0:T(8,128)(2,1)S(1)}, bf16[384,128]{1,0:T(8,128)(2,1)S(1)}, u32[]{:S(2)}, u32[]{:S(2)}) collective-permute-start(bf16[384,128]{1,0:T(8,128)(2,1)S(1)} %collective-permute-done.6.refs_3_), channel_id=1, source_target_pairs={{0,4},{4,0},{8,12},{12,8},{16,20},{20,16},{24,28},{28,24},{1,5},{5... | collective-permute-start | bytes 294920 | tf_op jit(solution)/shard_map/ppermute | solution.py:189
  16.9 5.6 %collective-permute-start.9 = (bf16[384,128]{1,0:T(8,128)(2,1)S(1)}, bf16[384,128]{1,0:T(8,128)(2,1)S(1)}, u32[]{:S(2)}, u32[]{:S(2)}) collective-permute-start(bf16[384,128]{1,0:T(8,128)(2,1)S(1)} %collective-permute-done.5.refs_2_), channel_id=1, source_target_pairs={{0,4},{4,0},{8,12},{12,8},{16,20},{20,16},{24,28},{28,24},{1,5},{5... | collective-permute-start | bytes 294920 | tf_op jit(solution)/shard_map/ppermute | solution.py:189
  17.0 5.5 %collective-permute-start.8 = (bf16[384,128]{1,0:T(8,128)(2,1)S(1)}, bf16[384,128]{1,0:T(8,128)(2,1)S(1)}, u32[]{:S(2)}, u32[]{:S(2)}) collective-permute-start(bf16[384,128]{1,0:T(8,128)(2,1)S(1)} %collective-permute-done.4.refs_1_), channel_id=1, source_target_pairs={{0,4},{4,0},{8,12},{12,8},{16,20},{20,16},{24,28},{28,24},{1,5},{5... | collective-permute-start | bytes 294920 | tf_op jit(solution)/shard_map/ppermute | solution.py:189

commit v2 on v1

v2 whole, which is shorter than its diff:
```python
import functools
import math

import jax
import jax.numpy as jnp
from jax import lax
from jax.experimental import pallas as pl
from jax.experimental.pallas import tpu as pltpu
from jax.sharding import PartitionSpec as P

BANDS = 3
BLOCKS = 4
LANES = 128
CORES = 2
COLUMNS_AT_ONCE = 8
VMEM = pl.BlockSpec(memory_space=pltpu.VMEM)
HBM = pl.BlockSpec(memory_space=pltpu.HBM)


def farthest(rank, plane, planes):
    mirrored = planes - 1 - plane
    if isinstance(plane, int) and isinstance(rank, int):
        alone, reach, outer = abs(plane - mirrored), min(plane, mirrored), rank if plane > mirrored else planes - 1 - rank
        pair = rank - alone
        inner = plane - (reach - pair // 2) if pair % 2 == 0 else plane + (reach - pair // 2)
        return outer if rank < alone else inner
    alone, reach = jnp.abs(plane - mirrored), jnp.minimum(plane, mirrored)
    outer = jnp.where(plane > mirrored, rank, planes - 1 - rank)
    pair = rank - alone
    away = reach - (pair >> 1)
    inner = jnp.where((pair & 1) == 0, plane - away, plane + away)
    return jnp.where(rank < alone, outer, inner)


def smoother(distance, owner, axis, length, offsets, masks, weights):
    matrix = jnp.where(distance == 0, jnp.float32(1.0), jnp.float32(0.0))
    for band in range(BANDS):
        value = masks[axis, band, 0].astype(jnp.float32) * weights[axis, band]
        for block in range(1, BLOCKS):
            here = masks[axis, band, block].astype(jnp.float32) * weights[axis, band]
            value = jnp.where(owner >= block * (length // BLOCKS), here, value)
        matrix = matrix + jnp.where(distance == offsets[axis, band], value, jnp.float32(0.0))
    return matrix.astype(jnp.bfloat16)


def write_columns(table, matrix, length):
    for place in range(length):
        table[place] = jnp.broadcast_to(matrix[:length, place : place + 1], (length, LANES))


def square_distance(length):
    row = lax.broadcasted_iota(jnp.int32, (LANES, LANES), 0)
    col = lax.broadcasted_iota(jnp.int32, (LANES, LANES), 1)
    return row, col, jnp.where((row < length) & (col < length), jnp.abs(row - col), -1)


def smooth_x_z(dims, field, out, blocks_z, table_x, along_z):
    length_x, width, depth = dims
    rows = COLUMNS_AT_ONCE * depth
    pieces = length_x * width // COLUMNS_AT_ONCE
    for first in range(0, pieces, 2):
        held = jnp.concatenate([field[piece * rows : (piece + 1) * rows, :] for piece in (first, first + 1)], axis=1)
        both = jnp.dot(blocks_z[...], held, preferred_element_type=jnp.float32)
        for piece in (0, 1):
            along_z[(first + piece) * rows : (first + piece + 1) * rows, :] = both[:, piece * LANES : (piece + 1) * LANES]
    slab = width * depth

    def one_x(x):
        total = table_x[0, pl.ds(x, 1), :] * along_z[0:slab, :]
        for other in range(1, length_x):
            total = total + table_x[other, pl.ds(x, 1), :] * along_z[other * slab : (other + 1) * slab, :]
        start = x * slab if isinstance(x, int) else pl.multiple_of(x * slab, 16)
        out[pl.ds(start, slab), :] = total.astype(jnp.bfloat16)

    if length_x <= 8:
        for x in range(length_x):
            one_x(x)
    else:
        pl.loop(0, length_x)(one_x)


def first_kernel(dims, length_y, *refs):
    length_x, width, depth = dims
    sources, (out, blocks_z, table_x, table_y) = refs[:4], refs[4:8]
    held, (along_z, arrivals) = refs[8:12], refs[12:]
    copies = [
        pltpu.make_async_copy(source, place, arrivals.at[which])
        for which, (source, place) in enumerate(zip(sources, held))
    ]
    for copy in copies:
        copy.start()
    for copy in copies[:3]:
        copy.wait()
    params, field = held[:3], held[3]
    row, col, distance = square_distance(length_x)
    write_columns(table_x, smoother(distance, row, 0, length_x, *params).astype(jnp.float32), length_x)
    row, col, distance = square_distance(length_y)
    gram = jnp.dot(
        smoother(distance, col, 1, length_y, *params),
        smoother(distance, row, 1, length_y, *params),
        preferred_element_type=jnp.float32,
    )
    write_columns(table_y, gram, length_y)
    rows = COLUMNS_AT_ONCE * depth
    shape = (COLUMNS_AT_ONCE, depth, rows)
    row_z = lax.broadcasted_iota(jnp.int32, shape, 1)
    row_group = lax.broadcasted_iota(jnp.int32, shape, 0)
    lane = lax.broadcasted_iota(jnp.int32, shape, 2)
    lane_group = jnp.zeros(shape, jnp.int32)
    for group in range(1, COLUMNS_AT_ONCE):
        lane_group = lane_group + jnp.where(lane >= group * depth, 1, 0)
    distance = jnp.where(row_group == lane_group, jnp.abs(row_z - (lane - lane_group * depth)), -1)
    matrix = smoother(distance, row_z, 2, depth, *params).astype(jnp.float32)
    blocks_z[...] = matrix.reshape(rows, rows).astype(jnp.bfloat16)
    copies[3].wait()
    smooth_x_z(dims, field, out, blocks_z, table_x, along_z)


def second_kernel(dims, field, blocks_z, table_x, out, along_z):
    smooth_x_z(dims, field, out, blocks_z, table_x, along_z)


def mix_y_kernel(dims, planes, table, *refs):
    length_x, width, depth = dims
    blocks, mine, (out, fields, mixed) = refs[:planes], refs[planes : 2 * planes], refs[2 * planes :]
    length_y = planes * width
    cells = length_x * width * depth
    plane = lax.axis_index("pencil")
    chip = lax.axis_index("dp") >> 1
    slabs = [farthest((chip ^ away) ^ plane, plane, planes) for away in range(planes)]

    def widen(block, slab):
        wide = block[...].astype(jnp.float32).reshape(length_x, width, depth, LANES)
        for y in range(width):
            fields[slab * width + y] = wide[:, y]

    @pl.when(chip == plane)
    def _():
        for away in range(planes):
            widen(mine[away], slabs[away])

    @pl.when(chip != plane)
    def _():
        for away in range(planes):
            widen(blocks[away], plane ^ away)

    def one_x(x, place, y):
        total = table[0, pl.ds(place, 1), :] * fields[0, x]
        for other in range(1, length_y):
            total = total + table[other, pl.ds(place, 1), :] * fields[other, x]
        start = (x * width + y) * depth
        mixed[pl.ds(start if isinstance(start, int) else pl.multiple_of(start, 8), depth), :] = total

    for away in range(planes):
        for y in range(width):
            place = slabs[away] * width + y
            if length_x <= 8:
                for x in range(length_x):
                    one_x(x, place, y)
            else:
                pl.loop(0, length_x)(functools.partial(one_x, place=place, y=y))
        for first in range(0, cells, LANES):
            out[away, :, first : first + LANES] = mixed[first : first + LANES, :].T.astype(jnp.bfloat16)


def gram_kernel(planes, mixed, *refs):
    mine, theirs, out = refs[:planes], refs[planes : 2 * planes], refs[2 * planes]
    total = None
    for away in range(planes):
        both = jnp.concatenate([mine[away][...], theirs[away][...]], axis=1)
        part = jnp.dot(mixed[away], both, preferred_element_type=jnp.float32)
        total = part if total is None else total + part
    core = lax.axis_index("dp") & 1
    out[:, pl.ds(pl.multiple_of(core * LANES, LANES), LANES)] = total[:, :LANES]
    out[:, pl.ds(pl.multiple_of((1 - core) * LANES, LANES), LANES)] = total[:, LANES:]


def call(kernel, out_shape, operands, in_specs, scratch=(), flops=0):
    sizes = jax.tree.leaves(out_shape) + list(operands)
    held = sum(item.size * item.dtype.itemsize for item in sizes)
    spare = sum(4 * math.prod(item.shape) for item in scratch if item.memory_space == pltpu.VMEM)
    return pl.pallas_call(
        kernel,
        out_shape=out_shape,
        in_specs=in_specs,
        out_specs=jax.tree.map(lambda _: VMEM, out_shape),
        scratch_shapes=list(scratch),
        compiler_params=pltpu.CompilerParams(vmem_limit_bytes=(6 << 20) + 2 * held + spare),
        cost_estimate=pl.CostEstimate(flops=flops, bytes_accessed=held, transcendentals=0),
    )(*operands)


def after(item, *others):
    return lax.optimization_barrier((item, *others))[0]


def shards(jacobian, band_offsets, band_masks, band_weights):
    length_x, width, depth, rows = jacobian.shape
    planes, spread = lax.axis_size("pencil"), lax.axis_size("dp")
    dims = (length_x, width, depth)
    cells = length_x * width * depth
    params = (band_offsets, band_masks, band_weights)
    field = jacobian.reshape(cells, rows)
    length_y = planes * width

    route = []
    for source in range(spread):
        for plane in range(planes):
            target_plane = source // CORES
            rank = [farthest(r, target_plane, planes) for r in range(planes)].index(plane)
            target = (target_plane ^ rank) * CORES + source % CORES
            route.append((source * planes + plane, target * planes + target_plane))
    arrived = lax.ppermute(field, ("dp", "pencil"), route)

    block = COLUMNS_AT_ONCE * depth
    smooth, blocks_z, table_x, table_y = call(
        functools.partial(first_kernel, dims, length_y),
        (
            jax.ShapeDtypeStruct((cells, rows), jnp.bfloat16),
            jax.ShapeDtypeStruct((block, block), jnp.bfloat16),
            jax.ShapeDtypeStruct((length_x, length_x, LANES), jnp.float32),
            jax.ShapeDtypeStruct((length_y, length_y, LANES), jnp.float32),
        ),
        tuple(pltpu.with_memory_space_constraint(item, pltpu.HBM) for item in (*params, field)),
        [HBM] * 4,
        [pltpu.SMEM(item.shape, item.dtype) for item in params]
        + [
            pltpu.VMEM((cells, rows), jnp.bfloat16),
            pltpu.VMEM((cells, LANES), jnp.float32),
            pltpu.SemaphoreType.DMA((4,)),
        ],
    )
    along = [smooth] + [None] * (planes - 1)
    for away in range(planes - 1, 0, -1):
        pairs = []
        for d in range(spread):
            for p in range(planes):
                needed = d // CORES != p ^ away
                target = (d, p ^ away) if needed else (p * CORES + d % CORES, p)
                pairs.append((d * planes + p, target[0] * planes + target[1]))
        along[away] = lax.ppermute(smooth, ("dp", "pencil"), pairs)
    mixed_arrived = call(
        functools.partial(second_kernel, dims),
        jax.ShapeDtypeStruct((cells, rows), jnp.bfloat16),
        (arrived, blocks_z, table_x),
        [VMEM] * 3,
        [pltpu.VMEM((cells, LANES), jnp.float32)],
    )
    mine = [mixed_arrived] + [
        lax.ppermute(mixed_arrived, "dp", [(i, i ^ (away * CORES)) for i in range(spread)]) for away in range(1, planes)
    ]
    theirs = []
    for which, item in enumerate(mine):
        item = after(item, *along[1:]) if which > 0 else item
        theirs.append(lax.ppermute(item, "dp", [(i, i ^ 1) for i in range(spread)]))
    mixed = call(
        functools.partial(mix_y_kernel, dims, planes),
        jax.ShapeDtypeStruct((planes, rows, cells), jnp.bfloat16),
        (table_y, *along, *mine),
        [VMEM] * (1 + 2 * planes),
        [
            pltpu.VMEM((length_y, length_x, depth, LANES), jnp.float32),
            pltpu.VMEM((cells, LANES), jnp.float32),
        ],
    )
    return call(
        functools.partial(gram_kernel, planes),
        jax.ShapeDtypeStruct((rows, CORES * rows), jnp.float32),
        (mixed, *mine, *theirs),
        [VMEM] * (1 + 2 * planes),
    )


def solution(mesh):
    in_specs = (P(None, "pencil", None, "dp"), P(), P(), P())
    out_specs = P("dp", "pencil")
    return jax.shard_map(shards, mesh=mesh, in_specs=in_specs, out_specs=out_specs, check_vma=False)
```

time: 23.7 us -> 21.6 us (0.911)
  the two profiles are of different devices: /device:TPU:14 before, /device:TPU:0 now
where the time goes in v2:
time: 21.6 us; the launch traced here: 21.5 us
  starting transfers between devices  13.5 us (62%)
  waiting for transfers between devices  4.76 us (22%)
  Pallas kernels  3.12 us (14%)
    ppermute x3, starting transfers between devices, shards(): lax.ppermute(mixed_arrived, 'dp', [(i, i ^ away * CORES) for i in range(s...  4.6 us
    ppermute x3, starting transfers between devices, shards(): along[away] = lax.ppermute(smooth, ('dp', 'pencil'), pairs)  4.52 us
    ppermute x3, waiting for transfers between devices, shards(): lax.ppermute(mixed_arrived, 'dp', [(i, i ^ away * CORES) for i in range(s...  4.4 us
    ppermute x1, starting transfers between devices, shards(): arrived = lax.ppermute(field, ('dp', 'pencil'), route)  3.89 us
    pallas_call x4, Pallas kernels, call(): pl.pallas_call(kernel, out_shape=out_shape, in_specs=in_specs, out_specs=...  3.12 us
    ppermute x4, starting transfers between devices, shards(): theirs.append(lax.ppermute(item, 'dp', [(i, i ^ 1) for i in range(spread)]))  0.52 us
  transfers between devices with their start and end apart: 11, of which 4 were waited for; matrix products, arithmetic and copies ran while one was open for 0% of the time, Pallas kernels for 10%

profile of v2, /device:TPU:0, one launch (start us, length us, event | category | flops | bytes accessed | tf_op | source)
XLA Modules:
  0.0 21.5 jit_solution(16854987938553214384)
XLA Ops:
  0.0 3.9 %collective-permute-start.3 = (bf16[384,128]{1,0:T(8,128)(2,1)}, bf16[384,128]{1,0:T(8,128)(2,1)S(1)}, u32[]{:S(2)}, u32[]{:S(2)}) collective-permute-start(bf16[384,128]{1,0:T(8,128)(2,1)} %bitcast.1), channel_id=1, source_target_pairs={{0,24},{1,16},{2,8},{3,0},{4,28},{5,20},{6,12},{7,4},{8,1},{9,17},... | collective-permute-start | bytes 294920 | tf_op jit(solution)/shard_map/ppermute | solution.py:213
  3.9 1.3 %shard_map.46 = (bf16[384,128]{1,0:T(8,128)(2,1)S(1)}, bf16[192,192]{1,0:T(8,128)(2,1)S(1)}, f32[8,8,128]{2,1,0:T(8,128)S(1)}, f32[8,8,128]{2,1,0:T(8,128)S(1)}) custom-call(s32[3,3]{1,0:T(4,128)} %refs_0_.1, s32[3,3,4]{2,1,0:T(4,128)} %refs_1_.1, f32[3,3]{1,0:T(4,128)} %refs_2_.1, bf16[384,128]{1,0:T(8,128)(2,1)} %bitcast.2), custom_call_target="tpu_custom_call" | custom-call | bytes 336088 | tf_op jit(solution)/shard_map/pallas_call | solution.py:182
  5.2 0.6 %collective-permute-start = (bf16[384,128]{1,0:T(8,128)(2,1)S(1)}, bf16[384,128]{1,0:T(8,128)(2,1)S(1)}, u32[]{:S(2)}, u32[]{:S(2)}) collective-permute-start(bf16[384,128]{1,0:T(8,128)(2,1)S(1)} %get-tuple-element.13.refs_0_), channel_id=1, source_target_pairs={{0,1},{1,9},{2,3},{3,2},{4,5},{5,13},{6,7},{7,6},{8,0},{9,8},{10,1... | collective-permute-start | bytes 294920 | tf_op jit(solution)/shard_map/ppermute | solution.py:241
  5.8 1.2 %collective-permute-start.1 = (bf16[384,128]{1,0:T(8,128)(2,1)S(1)}, bf16[384,128]{1,0:T(8,128)(2,1)S(1)}, u32[]{:S(2)}, u32[]{:S(2)}) collective-permute-start(bf16[384,128]{1,0:T(8,128)(2,1)S(1)} %get-tuple-element.13.refs_0_), channel_id=1, source_target_pairs={{0,2},{1,3},{2,18},{3,1},{4,6},{5,7},{6,22},{7,5},{8,10},{9,11},{1... | collective-permute-start | bytes 294920 | tf_op jit(solution)/shard_map/ppermute | solution.py:241
  7.0 2.8 %collective-permute-start.2 = (bf16[384,128]{1,0:T(8,128)(2,1)S(1)}, bf16[384,128]{1,0:T(8,128)(2,1)S(1)}, u32[]{:S(2)}, u32[]{:S(2)}) collective-permute-start(bf16[384,128]{1,0:T(8,128)(2,1)S(1)} %get-tuple-element.13.refs_0_), channel_id=1, source_target_pairs={{0,3},{1,2},{2,1},{3,27},{4,7},{5,6},{6,5},{7,31},{8,11},{9,10},{1... | collective-permute-start | bytes 294920 | tf_op jit(solution)/shard_map/ppermute | solution.py:241
  9.8 0.0 collective-permute-done.3.field
  9.8 0.3 %shard_map.47.refs_4_.refs_0_ = bf16[384,128]{1,0:T(8,128)(2,1)S(1)} custom-call(bf16[384,128]{1,0:T(8,128)(2,1)S(1)} %collective-permute-done.3.field, bf16[192,192]{1,0:T(8,128)(2,1)S(1)} %get-tuple-element.14.blocks_z, f32[8,8,128]{2,1,0:T(8,128)S(1)} %get-tuple-element.15.table_x), custom_call_target="tpu_custom_call" | custom-call | bytes 303104 | tf_op jit(solution)/shard_map/pallas_call | solution.py:182
  10.0 2.9 %collective-permute-start.4 = (bf16[384,128]{1,0:T(8,128)(2,1)S(1)}, bf16[384,128]{1,0:T(8,128)(2,1)S(1)}, u32[]{:S(2)}, u32[]{:S(2)}) collective-permute-start(bf16[384,128]{1,0:T(8,128)(2,1)S(1)} %shard_map.47.refs_4_.refs_0_), channel_id=1, source_target_pairs={{0,8},{4,12},{8,0},{12,4},{16,24},{20,28},{24,16},{28,20},{1,9},{5... | collective-permute-start | bytes 294920 | tf_op jit(solution)/shard_map/ppermute | solution.py:250
  12.9 0.4 %collective-permute-start.5 = (bf16[384,128]{1,0:T(8,128)(2,1)S(1)}, bf16[384,128]{1,0:T(8,128)(2,1)S(1)}, u32[]{:S(2)}, u32[]{:S(2)}) collective-permute-start(bf16[384,128]{1,0:T(8,128)(2,1)S(1)} %shard_map.47.refs_4_.refs_0_), channel_id=1, source_target_pairs={{0,16},{4,20},{8,24},{12,28},{16,0},{20,4},{24,8},{28,12},{1,17},{... | collective-permute-start | bytes 294920 | tf_op jit(solution)/shard_map/ppermute | solution.py:250
  13.2 0.0 collective-permute-done.refs_1_
  13.2 1.4 %collective-permute-start.6 = (bf16[384,128]{1,0:T(8,128)(2,1)S(1)}, bf16[384,128]{1,0:T(8,128)(2,1)S(1)}, u32[]{:S(2)}, u32[]{:S(2)}) collective-permute-start(bf16[384,128]{1,0:T(8,128)(2,1)S(1)} %shard_map.47.refs_4_.refs_0_), channel_id=1, source_target_pairs={{0,24},{4,28},{8,16},{12,20},{16,8},{20,12},{24,0},{28,4},{1,25},{... | collective-permute-start | bytes 294920 | tf_op jit(solution)/shard_map/ppermute | solution.py:250
  14.6 0.0 collective-permute-done.1.refs_2_
  14.6 0.0 collective-permute-start.7
  14.6 0.0 collective-permute-done.2.refs_3_
  14.6 1.3 %collective-permute-done.4.refs_5_.refs_1_ = bf16[384,128]{1,0:T(8,128)(2,1)S(1)} collective-permute-done((bf16[384,128]{1,0:T(8,128)(2,1)S(1)}, bf16[384,128]{1,0:T(8,128)(2,1)S(1)}, u32[]{:S(2)}, u32[]{:S(2)}) %collective-permute-start.4) | collective-permute-done | bytes 98336 | tf_op jit(solution)/shard_map/ppermute | solution.py:250
  16.0 0.0 collective-permute-start.8
  16.0 3.1 %collective-permute-done.5.refs_6_.refs_2_ = bf16[384,128]{1,0:T(8,128)(2,1)S(1)} collective-permute-done((bf16[384,128]{1,0:T(8,128)(2,1)S(1)}, bf16[384,128]{1,0:T(8,128)(2,1)S(1)}, u32[]{:S(2)}, u32[]{:S(2)}) %collective-permute-start.5) | collective-permute-done | bytes 98336 | tf_op jit(solution)/shard_map/ppermute | solution.py:250
  19.0 0.0 collective-permute-start.9
  19.0 0.0 collective-permute-done.6.refs_7_.refs_3_
  19.1 0.5 %collective-permute-start.10 = (bf16[384,128]{1,0:T(8,128)(2,1)S(1)}, bf16[384,128]{1,0:T(8,128)(2,1)S(1)}, u32[]{:S(2)}, u32[]{:S(2)}) collective-permute-start(bf16[384,128]{1,0:T(8,128)(2,1)S(1)} %collective-permute-done.6.refs_7_.refs_3_), channel_id=1, source_target_pairs={{0,4},{4,0},{8,12},{12,8},{16,20},{20,16},{24,28},{28,24},{1,5},{5... | collective-permute-start | bytes 294920 | tf_op jit(solution)/shard_map/ppermute | solution.py:255
  19.6 0.6 %shard_map.48.mixed = bf16[4,128,384]{2,1,0:T(8,128)(2,1)S(1)} custom-call(f32[8,8,128]{2,1,0:T(8,128)S(1)} %get-tuple-element.12.table, bf16[384,128]{1,0:T(8,128)(2,1)S(1)} %get-tuple-element.13.refs_0_, bf16[384,128]{1,0:T(8,128)(2,1)S(1)} %collective-permute-done.refs_1_, bf16[384,128]{1,0:T(8,128)(2,1)S(1)} %collective-permute-done.1.refs_2_, ...), custom_call_target="tpu_custom_call" | custom-call | bytes 1212416 | tf_op jit(solution)/shard_map/pallas_call | solution.py:182
  20.1 0.0 collective-permute-done.7.refs_4_
  20.1 0.0 collective-permute-done.8.refs_5_
  20.2 0.2 collective-permute-done.9.refs_6_
  20.3 0.2 collective-permute-done.10.refs_7_
  20.5 0.9 %shard_map.49 = f32[128,256]{1,0:T(8,128)} custom-call(bf16[4,128,384]{2,1,0:T(8,128)(2,1)S(1)} %shard_map.48.mixed, bf16[384,128]{1,0:T(8,128)(2,1)S(1)} %shard_map.47.refs_4_.refs_0_, bf16[384,128]{1,0:T(8,128)(2,1)S(1)} %collective-permute-done.4.refs_5_.refs_1_, bf16[384,128]{1,0:T(8,128)(2,1)S(1)} %collective-permute-done.5.refs_6_.refs_2_, ...), custom_call_target="tpu_custom_call" | custom-call | bytes 1310720 | tf_op jit(solution)/shard_map/pallas_call | solution.py:182
Async XLA Ops:
  0.0 9.8 %collective-permute-start.3 = (bf16[384,128]{1,0:T(8,128)(2,1)}, bf16[384,128]{1,0:T(8,128)(2,1)S(1)}, u32[]{:S(2)}, u32[]{:S(2)}) collective-permute-start(bf16[384,128]{1,0:T(8,128)(2,1)} %bitcast.1), channel_id=1, source_target_pairs={{0,24},{1,16},{2,8},{3,0},{4,28},{5,20},{6,12},{7,4},{8,1},{9,17},... | collective-permute-start | bytes 294920 | tf_op jit(solution)/shard_map/ppermute | solution.py:213
  5.2 8.0 %collective-permute-start = (bf16[384,128]{1,0:T(8,128)(2,1)S(1)}, bf16[384,128]{1,0:T(8,128)(2,1)S(1)}, u32[]{:S(2)}, u32[]{:S(2)}) collective-permute-start(bf16[384,128]{1,0:T(8,128)(2,1)S(1)} %get-tuple-element.13.refs_0_), channel_id=1, source_target_pairs={{0,1},{1,9},{2,3},{3,2},{4,5},{5,13},{6,7},{7,6},{8,0},{9,8},{10,1... | collective-permute-start | bytes 294920 | tf_op jit(solution)/shard_map/ppermute | solution.py:241
  5.8 8.8 %collective-permute-start.1 = (bf16[384,128]{1,0:T(8,128)(2,1)S(1)}, bf16[384,128]{1,0:T(8,128)(2,1)S(1)}, u32[]{:S(2)}, u32[]{:S(2)}) collective-permute-start(bf16[384,128]{1,0:T(8,128)(2,1)S(1)} %get-tuple-element.13.refs_0_), channel_id=1, source_target_pairs={{0,2},{1,3},{2,18},{3,1},{4,6},{5,7},{6,22},{7,5},{8,10},{9,11},{1... | collective-permute-start | bytes 294920 | tf_op jit(solution)/shard_map/ppermute | solution.py:241
  7.0 7.6 %collective-permute-start.2 = (bf16[384,128]{1,0:T(8,128)(2,1)S(1)}, bf16[384,128]{1,0:T(8,128)(2,1)S(1)}, u32[]{:S(2)}, u32[]{:S(2)}) collective-permute-start(bf16[384,128]{1,0:T(8,128)(2,1)S(1)} %get-tuple-element.13.refs_0_), channel_id=1, source_target_pairs={{0,3},{1,2},{2,1},{3,27},{4,7},{5,6},{6,5},{7,31},{8,11},{9,10},{1... | collective-permute-start | bytes 294920 | tf_op jit(solution)/shard_map/ppermute | solution.py:241
  10.0 5.9 %collective-permute-start.4 = (bf16[384,128]{1,0:T(8,128)(2,1)S(1)}, bf16[384,128]{1,0:T(8,128)(2,1)S(1)}, u32[]{:S(2)}, u32[]{:S(2)}) collective-permute-start(bf16[384,128]{1,0:T(8,128)(2,1)S(1)} %shard_map.47.refs_4_.refs_0_), channel_id=1, source_target_pairs={{0,8},{4,12},{8,0},{12,4},{16,24},{20,28},{24,16},{28,20},{1,9},{5... | collective-permute-start | bytes 294920 | tf_op jit(solution)/shard_map/ppermute | solution.py:250
  12.9 6.2 %collective-permute-start.5 = (bf16[384,128]{1,0:T(8,128)(2,1)S(1)}, bf16[384,128]{1,0:T(8,128)(2,1)S(1)}, u32[]{:S(2)}, u32[]{:S(2)}) collective-permute-start(bf16[384,128]{1,0:T(8,128)(2,1)S(1)} %shard_map.47.refs_4_.refs_0_), channel_id=1, source_target_pairs={{0,16},{4,20},{8,24},{12,28},{16,0},{20,4},{24,8},{28,12},{1,17},{... | collective-permute-start | bytes 294920 | tf_op jit(solution)/shard_map/ppermute | solution.py:250
  13.2 5.8 %collective-permute-start.6 = (bf16[384,128]{1,0:T(8,128)(2,1)S(1)}, bf16[384,128]{1,0:T(8,128)(2,1)S(1)}, u32[]{:S(2)}, u32[]{:S(2)}) collective-permute-start(bf16[384,128]{1,0:T(8,128)(2,1)S(1)} %shard_map.47.refs_4_.refs_0_), channel_id=1, source_target_pairs={{0,24},{4,28},{8,16},{12,20},{16,8},{20,12},{24,0},{28,4},{1,25},{... | collective-permute-start | bytes 294920 | tf_op jit(solution)/shard_map/ppermute | solution.py:250
  14.6 5.5 %collective-permute-start.7 = (bf16[384,128]{1,0:T(8,128)(2,1)S(1)}, bf16[384,128]{1,0:T(8,128)(2,1)S(1)}, u32[]{:S(2)}, u32[]{:S(2)}) collective-permute-start(bf16[384,128]{1,0:T(8,128)(2,1)S(1)} %shard_map.47.refs_4_.refs_0_), channel_id=1, source_target_pairs={{0,4},{4,0},{8,12},{12,8},{16,20},{20,16},{24,28},{28,24},{1,5},{5... | collective-permute-start | bytes 294920 | tf_op jit(solution)/shard_map/ppermute | solution.py:255
  16.0 4.2 %collective-permute-start.8 = (bf16[384,128]{1,0:T(8,128)(2,1)S(1)}, bf16[384,128]{1,0:T(8,128)(2,1)S(1)}, u32[]{:S(2)}, u32[]{:S(2)}) collective-permute-start(bf16[384,128]{1,0:T(8,128)(2,1)S(1)} %collective-permute-done.4.refs_5_.refs_1_), channel_id=1, source_target_pairs={{0,4},{4,0},{8,12},{12,8},{16,20},{20,16},{24,28},{28,24},{1,5},{5... | collective-permute-start | bytes 294920 | tf_op jit(solution)/shard_map/ppermute | solution.py:255
  19.0 1.3 %collective-permute-start.9 = (bf16[384,128]{1,0:T(8,128)(2,1)S(1)}, bf16[384,128]{1,0:T(8,128)(2,1)S(1)}, u32[]{:S(2)}, u32[]{:S(2)}) collective-permute-start(bf16[384,128]{1,0:T(8,128)(2,1)S(1)} %collective-permute-done.5.refs_6_.refs_2_), channel_id=1, source_target_pairs={{0,4},{4,0},{8,12},{12,8},{16,20},{20,16},{24,28},{28,24},{1,5},{5... | collective-permute-start | bytes 294920 | tf_op jit(solution)/shard_map/ppermute | solution.py:255
  19.1 1.5 %collective-permute-start.10 = (bf16[384,128]{1,0:T(8,128)(2,1)S(1)}, bf16[384,128]{1,0:T(8,128)(2,1)S(1)}, u32[]{:S(2)}, u32[]{:S(2)}) collective-permute-start(bf16[384,128]{1,0:T(8,128)(2,1)S(1)} %collective-permute-done.6.refs_7_.refs_3_), channel_id=1, source_target_pairs={{0,4},{4,0},{8,12},{12,8},{16,20},{20,16},{24,28},{28,24},{1,5},{5... | collective-permute-start | bytes 294920 | tf_op jit(solution)/shard_map/ppermute | solution.py:255

commit v3 on v2

--- a/solution.py
+++ b/solution.py
@@ -120,14 +120,14 @@
     smooth_x_z(dims, field, out, blocks_z, table_x, along_z)
 
 
-def mix_y_kernel(dims, planes, table, *refs):
+def mix_y_kernel(dims, planes, far_order, near_order, table, *refs):
     length_x, width, depth = dims
     blocks, mine, (out, fields, mixed) = refs[:planes], refs[planes : 2 * planes], refs[2 * planes :]
     length_y = planes * width
     cells = length_x * width * depth
     plane = lax.axis_index("pencil")
     chip = lax.axis_index("dp") >> 1
-    slabs = [farthest((chip ^ away) ^ plane, plane, planes) for away in range(planes)]
+    slabs = [farthest((chip ^ away) ^ plane, plane, planes) for away in near_order]
 
     def widen(block, slab):
         wide = block[...].astype(jnp.float32).reshape(length_x, width, depth, LANES)
@@ -136,13 +136,13 @@
 
     @pl.when(chip == plane)
     def _():
-        for away in range(planes):
-            widen(mine[away], slabs[away])
+        for block, slab in zip(mine, slabs):
+            widen(block, slab)
 
     @pl.when(chip != plane)
     def _():
-        for away in range(planes):
-            widen(blocks[away], plane ^ away)
+        for block, away in zip(blocks, far_order):
+            widen(block, plane ^ away)
 
     def one_x(x, place, y):
         total = table[0, pl.ds(place, 1), :] * fields[0, x]
@@ -230,15 +230,17 @@
             pltpu.SemaphoreType.DMA((4,)),
         ],
     )
-    along = [smooth] + [None] * (planes - 1)
-    for away in range(planes - 1, 0, -1):
+    far_order = (0, *range(1, planes, 2), *range(2, planes, 2))
+    near_order = (0, *range(planes - 1, 0, -1))
+    along = [smooth]
+    for away in far_order[1:]:
         pairs = []
         for d in range(spread):
             for p in range(planes):
                 needed = d // CORES != p ^ away
                 target = (d, p ^ away) if needed else (p * CORES + d % CORES, p)
                 pairs.append((d * planes + p, target[0] * planes + target[1]))
-        along[away] = lax.ppermute(smooth, ("dp", "pencil"), pairs)
+        along.append(lax.ppermute(smooth, ("dp", "pencil"), pairs))
     mixed_arrived = call(
         functools.partial(second_kernel, dims),
         jax.ShapeDtypeStruct((cells, rows), jnp.bfloat16),
@@ -247,14 +249,14 @@
         [pltpu.VMEM((cells, LANES), jnp.float32)],
     )
     mine = [mixed_arrived] + [
-        lax.ppermute(mixed_arrived, "dp", [(i, i ^ (away * CORES)) for i in range(spread)]) for away in range(1, planes)
+        lax.ppermute(mixed_arrived, "dp", [(i, i ^ (away * CORES)) for i in range(spread)]) for away in near_order[1:]
     ]
     theirs = []
     for which, item in enumerate(mine):
         item = after(item, *along[1:]) if which > 0 else item
         theirs.append(lax.ppermute(item, "dp", [(i, i ^ 1) for i in range(spread)]))
     mixed = call(
-        functools.partial(mix_y_kernel, dims, planes),
+        functools.partial(mix_y_kernel, dims, planes, far_order, near_order),
         jax.ShapeDtypeStruct((planes, rows, cells), jnp.bfloat16),
         (table_y, *along, *mine),
         [VMEM] * (1 + 2 * planes),

time: 21.6 us -> 21 us (0.972)
  starting transfers between devices: 13.5 us -> 13 us
    ppermute x3, waiting for transfers between devices: 4.4 us -> 2.27 us  [shards(): lax.ppermute(mixed_arrived, 'dp', [(i, i ^ away * CORES) for i in range(s...]
    ppermute x3, waiting for transfers between devices: 0.01 us -> 1.7 us  [shards(): along.append(lax.ppermute(smooth, ('dp', 'pencil'), pairs))]
    ppermute x3, starting transfers between devices: 4.6 us -> 5.5 us  [shards(): lax.ppermute(mixed_arrived, 'dp', [(i, i ^ away * CORES) for i in range(s...]
    ppermute x3, starting transfers between devices: 4.52 us -> 3.62 us  [shards(): along.append(lax.ppermute(smooth, ('dp', 'pencil'), pairs))]
    ppermute x4, starting transfers between devices: 0.52 us -> 0.01 us  [shards(): theirs.append(lax.ppermute(item, 'dp', [(i, i ^ 1) for i in range(spread)]))]
    ppermute x4, waiting for transfers between devices: 0.35 us -> 0.71 us  [shards(): theirs.append(lax.ppermute(item, 'dp', [(i, i ^ 1) for i in range(spread)]))]
  transfers between devices with their start and end apart: 11 -> 11, of which waited for: 4 -> 5; matrix products, arithmetic and copies ran while one was open for 0% -> 0% of each run, Pallas kernels for 10% -> 10%
where the time goes in v3:
time: 21 us; the launch traced here: 20.9 us
  starting transfers between devices  13 us (62%)
  waiting for transfers between devices  4.68 us (22%)
  Pallas kernels  3.12 us (15%)
    ppermute x3, starting transfers between devices, shards(): lax.ppermute(mixed_arrived, 'dp', [(i, i ^ away * CORES) for i in range(s...  5.5 us
    ppermute x1, starting transfers between devices, shards(): arrived = lax.ppermute(field, ('dp', 'pencil'), route)  3.89 us
    ppermute x3, starting transfers between devices, shards(): along.append(lax.ppermute(smooth, ('dp', 'pencil'), pairs))  3.62 us
    pallas_call x4, Pallas kernels, call(): pl.pallas_call(kernel, out_shape=out_shape, in_specs=in_specs, out_specs=...  3.12 us
    ppermute x3, waiting for transfers between devices, shards(): lax.ppermute(mixed_arrived, 'dp', [(i, i ^ away * CORES) for i in range(s...  2.27 us
    ppermute x3, waiting for transfers between devices, shards(): along.append(lax.ppermute(smooth, ('dp', 'pencil'), pairs))  1.7 us
    ppermute x4, waiting for transfers between devices, shards(): theirs.append(lax.ppermute(item, 'dp', [(i, i ^ 1) for i in range(spread)]))  0.71 us
  transfers between devices with their start and end apart: 11, of which 5 were waited for; matrix products, arithmetic and copies ran while one was open for 0% of the time, Pallas kernels for 10%

profile of v3, /device:TPU:0, one launch (start us, length us, event | category | flops | bytes accessed | tf_op | source)
XLA Modules:
  0.0 20.9 jit_solution(16379694669962883832)
XLA Ops:
  0.0 3.9 %collective-permute-start.3 = (bf16[384,128]{1,0:T(8,128)(2,1)}, bf16[384,128]{1,0:T(8,128)(2,1)S(1)}, u32[]{:S(2)}, u32[]{:S(2)}) collective-permute-start(bf16[384,128]{1,0:T(8,128)(2,1)} %bitcast.1), channel_id=1, source_target_pairs={{0,24},{1,16},{2,8},{3,0},{4,28},{5,20},{6,12},{7,4},{8,1},{9,17},... | collective-permute-start | bytes 294920 | tf_op jit(solution)/shard_map/ppermute | solution.py:213
  3.9 1.3 %shard_map.46 = (bf16[384,128]{1,0:T(8,128)(2,1)S(1)}, bf16[192,192]{1,0:T(8,128)(2,1)S(1)}, f32[8,8,128]{2,1,0:T(8,128)S(1)}, f32[8,8,128]{2,1,0:T(8,128)S(1)}) custom-call(s32[3,3]{1,0:T(4,128)} %refs_0_.1, s32[3,3,4]{2,1,0:T(4,128)} %refs_1_.1, f32[3,3]{1,0:T(4,128)} %refs_2_.1, bf16[384,128]{1,0:T(8,128)(2,1)} %bitcast.2), custom_call_target="tpu_custom_call" | custom-call | bytes 336088 | tf_op jit(solution)/shard_map/pallas_call | solution.py:182
  5.2 0.6 %collective-permute-start = (bf16[384,128]{1,0:T(8,128)(2,1)S(1)}, bf16[384,128]{1,0:T(8,128)(2,1)S(1)}, u32[]{:S(2)}, u32[]{:S(2)}) collective-permute-start(bf16[384,128]{1,0:T(8,128)(2,1)S(1)} %get-tuple-element.13.refs_0_), channel_id=1, source_target_pairs={{0,1},{1,9},{2,3},{3,2},{4,5},{5,13},{6,7},{7,6},{8,0},{9,8},{10,1... | collective-permute-start | bytes 294920 | tf_op jit(solution)/shard_map/ppermute | solution.py:243
  5.8 2.3 %collective-permute-start.1 = (bf16[384,128]{1,0:T(8,128)(2,1)S(1)}, bf16[384,128]{1,0:T(8,128)(2,1)S(1)}, u32[]{:S(2)}, u32[]{:S(2)}) collective-permute-start(bf16[384,128]{1,0:T(8,128)(2,1)S(1)} %get-tuple-element.13.refs_0_), channel_id=1, source_target_pairs={{0,3},{1,2},{2,1},{3,27},{4,7},{5,6},{6,5},{7,31},{8,11},{9,10},{1... | collective-permute-start | bytes 294920 | tf_op jit(solution)/shard_map/ppermute | solution.py:243
  8.1 0.7 %collective-permute-start.2 = (bf16[384,128]{1,0:T(8,128)(2,1)S(1)}, bf16[384,128]{1,0:T(8,128)(2,1)S(1)}, u32[]{:S(2)}, u32[]{:S(2)}) collective-permute-start(bf16[384,128]{1,0:T(8,128)(2,1)S(1)} %get-tuple-element.13.refs_0_), channel_id=1, source_target_pairs={{0,2},{1,3},{2,18},{3,1},{4,6},{5,7},{6,22},{7,5},{8,10},{9,11},{1... | collective-permute-start | bytes 294920 | tf_op jit(solution)/shard_map/ppermute | solution.py:243
  8.9 0.0 collective-permute-done.3.field
  8.9 0.3 %shard_map.47.refs_4_.refs_0_ = bf16[384,128]{1,0:T(8,128)(2,1)S(1)} custom-call(bf16[384,128]{1,0:T(8,128)(2,1)S(1)} %collective-permute-done.3.field, bf16[192,192]{1,0:T(8,128)(2,1)S(1)} %get-tuple-element.14.blocks_z, f32[8,8,128]{2,1,0:T(8,128)S(1)} %get-tuple-element.15.table_x), custom_call_target="tpu_custom_call" | custom-call | bytes 303104 | tf_op jit(solution)/shard_map/pallas_call | solution.py:182
  9.1 3.6 %collective-permute-start.4 = (bf16[384,128]{1,0:T(8,128)(2,1)S(1)}, bf16[384,128]{1,0:T(8,128)(2,1)S(1)}, u32[]{:S(2)}, u32[]{:S(2)}) collective-permute-start(bf16[384,128]{1,0:T(8,128)(2,1)S(1)} %shard_map.47.refs_4_.refs_0_), channel_id=1, source_target_pairs={{0,24},{4,28},{8,16},{12,20},{16,8},{20,12},{24,0},{28,4},{1,25},{... | collective-permute-start | bytes 294920 | tf_op jit(solution)/shard_map/ppermute | solution.py:252
  12.7 0.8 %collective-permute-start.5 = (bf16[384,128]{1,0:T(8,128)(2,1)S(1)}, bf16[384,128]{1,0:T(8,128)(2,1)S(1)}, u32[]{:S(2)}, u32[]{:S(2)}) collective-permute-start(bf16[384,128]{1,0:T(8,128)(2,1)S(1)} %shard_map.47.refs_4_.refs_0_), channel_id=1, source_target_pairs={{0,16},{4,20},{8,24},{12,28},{16,0},{20,4},{24,8},{28,12},{1,17},{... | collective-permute-start | bytes 294920 | tf_op jit(solution)/shard_map/ppermute | solution.py:252
  13.6 0.0 collective-permute-done.refs_1_
  13.6 1.1 %collective-permute-start.6 = (bf16[384,128]{1,0:T(8,128)(2,1)S(1)}, bf16[384,128]{1,0:T(8,128)(2,1)S(1)}, u32[]{:S(2)}, u32[]{:S(2)}) collective-permute-start(bf16[384,128]{1,0:T(8,128)(2,1)S(1)} %shard_map.47.refs_4_.refs_0_), channel_id=1, source_target_pairs={{0,8},{4,12},{8,0},{12,4},{16,24},{20,28},{24,16},{28,20},{1,9},{5... | collective-permute-start | bytes 294920 | tf_op jit(solution)/shard_map/ppermute | solution.py:252
  14.6 0.0 collective-permute-done.1.refs_2_
  14.6 0.0 collective-permute-start.7
  14.6 1.7 %collective-permute-done.2.refs_3_ = bf16[384,128]{1,0:T(8,128)(2,1)S(1)} collective-permute-done((bf16[384,128]{1,0:T(8,128)(2,1)S(1)}, bf16[384,128]{1,0:T(8,128)(2,1)S(1)}, u32[]{:S(2)}, u32[]{:S(2)}) %collective-permute-start.2) | collective-permute-done | bytes 98336 | tf_op jit(solution)/shard_map/ppermute | solution.py:243
  16.3 0.0 collective-permute-done.4.refs_5_.refs_1_
  16.3 0.0 collective-permute-start.8
  16.3 1.6 %collective-permute-done.5.refs_6_.refs_2_ = bf16[384,128]{1,0:T(8,128)(2,1)S(1)} collective-permute-done((bf16[384,128]{1,0:T(8,128)(2,1)S(1)}, bf16[384,128]{1,0:T(8,128)(2,1)S(1)}, u32[]{:S(2)}, u32[]{:S(2)}) %collective-permute-start.5) | collective-permute-done | bytes 98336 | tf_op jit(solution)/shard_map/ppermute | solution.py:252
  18.0 0.0 collective-permute-start.9
  18.0 0.6 %collective-permute-done.6.refs_7_.refs_3_ = bf16[384,128]{1,0:T(8,128)(2,1)S(1)} collective-permute-done((bf16[384,128]{1,0:T(8,128)(2,1)S(1)}, bf16[384,128]{1,0:T(8,128)(2,1)S(1)}, u32[]{:S(2)}, u32[]{:S(2)}) %collective-permute-start.6) | collective-permute-done | bytes 98336 | tf_op jit(solution)/shard_map/ppermute | solution.py:252
  18.6 0.0 collective-permute-start.10
  18.6 0.6 %shard_map.48.mixed = bf16[4,128,384]{2,1,0:T(8,128)(2,1)S(1)} custom-call(f32[8,8,128]{2,1,0:T(8,128)S(1)} %get-tuple-element.12.table, bf16[384,128]{1,0:T(8,128)(2,1)S(1)} %get-tuple-element.13.refs_0_, bf16[384,128]{1,0:T(8,128)(2,1)S(1)} %collective-permute-done.refs_1_, bf16[384,128]{1,0:T(8,128)(2,1)S(1)} %collective-permute-done.1.refs_2_, ...), custom_call_target="tpu_custom_call" | custom-call | bytes 1212416 | tf_op jit(solution)/shard_map/pallas_call | solution.py:182
  19.2 0.0 collective-permute-done.7.refs_4_
  19.2 0.0 collective-permute-done.8.refs_5_
  19.2 0.1 collective-permute-done.9.refs_6_
  19.3 0.6 %collective-permute-done.10.refs_7_ = bf16[384,128]{1,0:T(8,128)(2,1)S(1)} collective-permute-done((bf16[384,128]{1,0:T(8,128)(2,1)S(1)}, bf16[384,128]{1,0:T(8,128)(2,1)S(1)}, u32[]{:S(2)}, u32[]{:S(2)}) %collective-permute-start.10) | collective-permute-done | bytes 98336 | tf_op jit(solution)/shard_map/ppermute | solution.py:257
  19.9 0.9 %shard_map.49 = f32[128,256]{1,0:T(8,128)} custom-call(bf16[4,128,384]{2,1,0:T(8,128)(2,1)S(1)} %shard_map.48.mixed, bf16[384,128]{1,0:T(8,128)(2,1)S(1)} %shard_map.47.refs_4_.refs_0_, bf16[384,128]{1,0:T(8,128)(2,1)S(1)} %collective-permute-done.4.refs_5_.refs_1_, bf16[384,128]{1,0:T(8,128)(2,1)S(1)} %collective-permute-done.5.refs_6_.refs_2_, ...), custom_call_target="tpu_custom_call" | custom-call | bytes 1310720 | tf_op jit(solution)/shard_map/pallas_call | solution.py:182
Async XLA Ops:
  0.0 8.9 %collective-permute-start.3 = (bf16[384,128]{1,0:T(8,128)(2,1)}, bf16[384,128]{1,0:T(8,128)(2,1)S(1)}, u32[]{:S(2)}, u32[]{:S(2)}) collective-permute-start(bf16[384,128]{1,0:T(8,128)(2,1)} %bitcast.1), channel_id=1, source_target_pairs={{0,24},{1,16},{2,8},{3,0},{4,28},{5,20},{6,12},{7,4},{8,1},{9,17},... | collective-permute-start | bytes 294920 | tf_op jit(solution)/shard_map/ppermute | solution.py:213
  5.2 8.3 %collective-permute-start = (bf16[384,128]{1,0:T(8,128)(2,1)S(1)}, bf16[384,128]{1,0:T(8,128)(2,1)S(1)}, u32[]{:S(2)}, u32[]{:S(2)}) collective-permute-start(bf16[384,128]{1,0:T(8,128)(2,1)S(1)} %get-tuple-element.13.refs_0_), channel_id=1, source_target_pairs={{0,1},{1,9},{2,3},{3,2},{4,5},{5,13},{6,7},{7,6},{8,0},{9,8},{10,1... | collective-permute-start | bytes 294920 | tf_op jit(solution)/shard_map/ppermute | solution.py:243
  5.8 8.8 %collective-permute-start.1 = (bf16[384,128]{1,0:T(8,128)(2,1)S(1)}, bf16[384,128]{1,0:T(8,128)(2,1)S(1)}, u32[]{:S(2)}, u32[]{:S(2)}) collective-permute-start(bf16[384,128]{1,0:T(8,128)(2,1)S(1)} %get-tuple-element.13.refs_0_), channel_id=1, source_target_pairs={{0,3},{1,2},{2,1},{3,27},{4,7},{5,6},{6,5},{7,31},{8,11},{9,10},{1... | collective-permute-start | bytes 294920 | tf_op jit(solution)/shard_map/ppermute | solution.py:243
  8.1 8.2 %collective-permute-start.2 = (bf16[384,128]{1,0:T(8,128)(2,1)S(1)}, bf16[384,128]{1,0:T(8,128)(2,1)S(1)}, u32[]{:S(2)}, u32[]{:S(2)}) collective-permute-start(bf16[384,128]{1,0:T(8,128)(2,1)S(1)} %get-tuple-element.13.refs_0_), channel_id=1, source_target_pairs={{0,2},{1,3},{2,18},{3,1},{4,6},{5,7},{6,22},{7,5},{8,10},{9,11},{1... | collective-permute-start | bytes 294920 | tf_op jit(solution)/shard_map/ppermute | solution.py:243
  9.1 7.2 %collective-permute-start.4 = (bf16[384,128]{1,0:T(8,128)(2,1)S(1)}, bf16[384,128]{1,0:T(8,128)(2,1)S(1)}, u32[]{:S(2)}, u32[]{:S(2)}) collective-permute-start(bf16[384,128]{1,0:T(8,128)(2,1)S(1)} %shard_map.47.refs_4_.refs_0_), channel_id=1, source_target_pairs={{0,24},{4,28},{8,16},{12,20},{16,8},{20,12},{24,0},{28,4},{1,25},{... | collective-permute-start | bytes 294920 | tf_op jit(solution)/shard_map/ppermute | solution.py:252
  12.7 5.3 %collective-permute-start.5 = (bf16[384,128]{1,0:T(8,128)(2,1)S(1)}, bf16[384,128]{1,0:T(8,128)(2,1)S(1)}, u32[]{:S(2)}, u32[]{:S(2)}) collective-permute-start(bf16[384,128]{1,0:T(8,128)(2,1)S(1)} %shard_map.47.refs_4_.refs_0_), channel_id=1, source_target_pairs={{0,16},{4,20},{8,24},{12,28},{16,0},{20,4},{24,8},{28,12},{1,17},{... | collective-permute-start | bytes 294920 | tf_op jit(solution)/shard_map/ppermute | solution.py:252
  13.6 5.1 %collective-permute-start.6 = (bf16[384,128]{1,0:T(8,128)(2,1)S(1)}, bf16[384,128]{1,0:T(8,128)(2,1)S(1)}, u32[]{:S(2)}, u32[]{:S(2)}) collective-permute-start(bf16[384,128]{1,0:T(8,128)(2,1)S(1)} %shard_map.47.refs_4_.refs_0_), channel_id=1, source_target_pairs={{0,8},{4,12},{8,0},{12,4},{16,24},{20,28},{24,16},{28,20},{1,9},{5... | collective-permute-start | bytes 294920 | tf_op jit(solution)/shard_map/ppermute | solution.py:252
  14.6 4.6 %collective-permute-start.7 = (bf16[384,128]{1,0:T(8,128)(2,1)S(1)}, bf16[384,128]{1,0:T(8,128)(2,1)S(1)}, u32[]{:S(2)}, u32[]{:S(2)}) collective-permute-start(bf16[384,128]{1,0:T(8,128)(2,1)S(1)} %shard_map.47.refs_4_.refs_0_), channel_id=1, source_target_pairs={{0,4},{4,0},{8,12},{12,8},{16,20},{20,16},{24,28},{28,24},{1,5},{5... | collective-permute-start | bytes 294920 | tf_op jit(solution)/shard_map/ppermute | solution.py:257
  16.3 2.9 %collective-permute-start.8 = (bf16[384,128]{1,0:T(8,128)(2,1)S(1)}, bf16[384,128]{1,0:T(8,128)(2,1)S(1)}, u32[]{:S(2)}, u32[]{:S(2)}) collective-permute-start(bf16[384,128]{1,0:T(8,128)(2,1)S(1)} %collective-permute-done.4.refs_5_.refs_1_), channel_id=1, source_target_pairs={{0,4},{4,0},{8,12},{12,8},{16,20},{20,16},{24,28},{28,24},{1,5},{5... | collective-permute-start | bytes 294920 | tf_op jit(solution)/shard_map/ppermute | solution.py:257
  18.0 1.3 %collective-permute-start.9 = (bf16[384,128]{1,0:T(8,128)(2,1)S(1)}, bf16[384,128]{1,0:T(8,128)(2,1)S(1)}, u32[]{:S(2)}, u32[]{:S(2)}) collective-permute-start(bf16[384,128]{1,0:T(8,128)(2,1)S(1)} %collective-permute-done.5.refs_6_.refs_2_), channel_id=1, source_target_pairs={{0,4},{4,0},{8,12},{12,8},{16,20},{20,16},{24,28},{28,24},{1,5},{5... | collective-permute-start | bytes 294920 | tf_op jit(solution)/shard_map/ppermute | solution.py:257
  18.6 1.3 %collective-permute-start.10 = (bf16[384,128]{1,0:T(8,128)(2,1)S(1)}, bf16[384,128]{1,0:T(8,128)(2,1)S(1)}, u32[]{:S(2)}, u32[]{:S(2)}) collective-permute-start(bf16[384,128]{1,0:T(8,128)(2,1)S(1)} %collective-permute-done.6.refs_7_.refs_3_), channel_id=1, source_target_pairs={{0,4},{4,0},{8,12},{12,8},{16,20},{20,16},{24,28},{28,24},{1,5},{5... | collective-permute-start | bytes 294920 | tf_op jit(solution)/shard_map/ppermute | solution.py:257

commit v4 on v3

--- a/solution.py
+++ b/solution.py
@@ -9,6 +9,7 @@
 from jax.sharding import PartitionSpec as P
 
 BANDS = 3
+PLACES = (3, 2, 0, 1)
 BLOCKS = 4
 LANES = 128
 CORES = 2
@@ -30,6 +31,13 @@
     away = reach - (pair >> 1)
     inner = jnp.where((pair & 1) == 0, plane - away, plane + away)
     return jnp.where(rank < alone, outer, inner)
+
+
+def decode(value):
+    rank = value
+    for which, code in enumerate(PLACES):
+        rank = jnp.where(value == code, which, rank)
+    return rank
 
 
 def smoother(distance, owner, axis, length, offsets, masks, weights):
@@ -127,7 +135,7 @@
     cells = length_x * width * depth
     plane = lax.axis_index("pencil")
     chip = lax.axis_index("dp") >> 1
-    slabs = [farthest((chip ^ away) ^ plane, plane, planes) for away in near_order]
+    slabs = [farthest(decode((chip ^ away) ^ plane), plane, planes) for away in near_order]
 
     def widen(block, slab):
         wide = block[...].astype(jnp.float32).reshape(length_x, width, depth, LANES)
@@ -208,7 +216,7 @@
         for plane in range(planes):
             target_plane = source // CORES
             rank = [farthest(r, target_plane, planes) for r in range(planes)].index(plane)
-            target = (target_plane ^ rank) * CORES + source % CORES
+            target = (target_plane ^ (PLACES[rank] if rank < len(PLACES) else rank)) * CORES + source % CORES
             route.append((source * planes + plane, target * planes + target_plane))
     arrived = lax.ppermute(field, ("dp", "pencil"), route)
 
@@ -231,7 +239,7 @@
         ],
     )
     far_order = (0, *range(1, planes, 2), *range(2, planes, 2))
-    near_order = (0, *range(planes - 1, 0, -1))
+    near_order = far_order
     along = [smooth]
     for away in far_order[1:]:
         pairs = []

time: 21 us -> 20.8 us (level)
  starting transfers between devices: 13 us -> 12.6 us
    ppermute x3, starting transfers between devices: 3.62 us -> 4.83 us  [shards(): along.append(lax.ppermute(smooth, ('dp', 'pencil'), pairs))]
    ppermute x3, waiting for transfers between devices: 2.27 us -> 3.37 us  [shards(): lax.ppermute(mixed_arrived, 'dp', [(i, i ^ away * CORES) for i in range(s...]
    ppermute x1, starting transfers between devices: 3.89 us -> 2.94 us  [shards(): arrived = lax.ppermute(field, ('dp', 'pencil'), route)]
    ppermute x3, waiting for transfers between devices: 1.7 us -> 0.76 us  [shards(): along.append(lax.ppermute(smooth, ('dp', 'pencil'), pairs))]
    ppermute x3, starting transfers between devices: 5.5 us -> 4.84 us  [shards(): lax.ppermute(mixed_arrived, 'dp', [(i, i ^ away * CORES) for i in range(s...]
  transfers between devices with their start and end apart: 11 -> 11, of which waited for: 5 -> 4; matrix products, arithmetic and copies ran while one was open for 0% -> 0% of each run, Pallas kernels for 10% -> 11%
where the time goes in v4:
time: 20.8 us; the launch traced here: 20.6 us
  starting transfers between devices  12.6 us (61%)
  waiting for transfers between devices  4.83 us (23%)
  Pallas kernels  3.11 us (15%)
    ppermute x3, starting transfers between devices, shards(): lax.ppermute(mixed_arrived, 'dp', [(i, i ^ away * CORES) for i in range(s...  4.84 us
    ppermute x3, starting transfers between devices, shards(): along.append(lax.ppermute(smooth, ('dp', 'pencil'), pairs))  4.83 us
    ppermute x3, waiting for transfers between devices, shards(): lax.ppermute(mixed_arrived, 'dp', [(i, i ^ away * CORES) for i in range(s...  3.37 us
    pallas_call x4, Pallas kernels, call(): pl.pallas_call(kernel, out_shape=out_shape, in_specs=in_specs, out_specs=...  3.11 us
    ppermute x1, starting transfers between devices, shards(): arrived = lax.ppermute(field, ('dp', 'pencil'), route)  2.94 us
    ppermute x3, waiting for transfers between devices, shards(): along.append(lax.ppermute(smooth, ('dp', 'pencil'), pairs))  0.76 us
    ppermute x4, waiting for transfers between devices, shards(): theirs.append(lax.ppermute(item, 'dp', [(i, i ^ 1) for i in range(spread)]))  0.7 us
  transfers between devices with their start and end apart: 11, of which 4 were waited for; matrix products, arithmetic and copies ran while one was open for 0% of the time, Pallas kernels for 11%

profile of v4, /device:TPU:0, one launch (start us, length us, event | category | flops | bytes accessed | tf_op | source)
XLA Modules:
  0.0 20.6 jit_solution(10003820144998187288)
XLA Ops:
  0.0 2.9 %collective-permute-start.3 = (bf16[384,128]{1,0:T(8,128)(2,1)}, bf16[384,128]{1,0:T(8,128)(2,1)S(1)}, u32[]{:S(2)}, u32[]{:S(2)}) collective-permute-start(bf16[384,128]{1,0:T(8,128)(2,1)} %bitcast.1), channel_id=1, source_target_pairs={{0,8},{1,0},{2,16},{3,24},{4,12},{5,4},{6,20},{7,28},{8,25},{9,1},... | collective-permute-start | bytes 294920 | tf_op jit(solution)/shard_map/ppermute | solution.py:221
  2.9 1.3 %shard_map.46 = (bf16[384,128]{1,0:T(8,128)(2,1)S(1)}, bf16[192,192]{1,0:T(8,128)(2,1)S(1)}, f32[8,8,128]{2,1,0:T(8,128)S(1)}, f32[8,8,128]{2,1,0:T(8,128)S(1)}) custom-call(s32[3,3]{1,0:T(4,128)} %refs_0_.1, s32[3,3,4]{2,1,0:T(4,128)} %refs_1_.1, f32[3,3]{1,0:T(4,128)} %refs_2_.1, bf16[384,128]{1,0:T(8,128)(2,1)} %bitcast.2), custom_call_target="tpu_custom_call" | custom-call | bytes 336088 | tf_op jit(solution)/shard_map/pallas_call | solution.py:190
  4.3 0.1 collective-permute-start
  4.4 4.2 %collective-permute-start.1 = (bf16[384,128]{1,0:T(8,128)(2,1)S(1)}, bf16[384,128]{1,0:T(8,128)(2,1)S(1)}, u32[]{:S(2)}, u32[]{:S(2)}) collective-permute-start(bf16[384,128]{1,0:T(8,128)(2,1)S(1)} %get-tuple-element.13.refs_0_), channel_id=1, source_target_pairs={{0,3},{1,2},{2,1},{3,27},{4,7},{5,6},{6,5},{7,31},{8,11},{9,10},{1... | collective-permute-start | bytes 294920 | tf_op jit(solution)/shard_map/ppermute | solution.py:251
  8.6 0.5 %collective-permute-start.2 = (bf16[384,128]{1,0:T(8,128)(2,1)S(1)}, bf16[384,128]{1,0:T(8,128)(2,1)S(1)}, u32[]{:S(2)}, u32[]{:S(2)}) collective-permute-start(bf16[384,128]{1,0:T(8,128)(2,1)S(1)} %get-tuple-element.13.refs_0_), channel_id=1, source_target_pairs={{0,2},{1,3},{2,18},{3,1},{4,6},{5,7},{6,22},{7,5},{8,10},{9,11},{1... | collective-permute-start | bytes 294920 | tf_op jit(solution)/shard_map/ppermute | solution.py:251
  9.1 0.0 collective-permute-done.3.field
  9.1 0.3 %shard_map.47.refs_4_.refs_0_ = bf16[384,128]{1,0:T(8,128)(2,1)S(1)} custom-call(bf16[384,128]{1,0:T(8,128)(2,1)S(1)} %collective-permute-done.3.field, bf16[192,192]{1,0:T(8,128)(2,1)S(1)} %get-tuple-element.14.blocks_z, f32[8,8,128]{2,1,0:T(8,128)S(1)} %get-tuple-element.15.table_x), custom_call_target="tpu_custom_call" | custom-call | bytes 303104 | tf_op jit(solution)/shard_map/pallas_call | solution.py:190
  9.4 1.4 %collective-permute-start.4 = (bf16[384,128]{1,0:T(8,128)(2,1)S(1)}, bf16[384,128]{1,0:T(8,128)(2,1)S(1)}, u32[]{:S(2)}, u32[]{:S(2)}) collective-permute-start(bf16[384,128]{1,0:T(8,128)(2,1)S(1)} %shard_map.47.refs_4_.refs_0_), channel_id=1, source_target_pairs={{0,8},{4,12},{8,0},{12,4},{16,24},{20,28},{24,16},{28,20},{1,9},{5... | collective-permute-start | bytes 294920 | tf_op jit(solution)/shard_map/ppermute | solution.py:260
  10.8 3.0 %collective-permute-start.5 = (bf16[384,128]{1,0:T(8,128)(2,1)S(1)}, bf16[384,128]{1,0:T(8,128)(2,1)S(1)}, u32[]{:S(2)}, u32[]{:S(2)}) collective-permute-start(bf16[384,128]{1,0:T(8,128)(2,1)S(1)} %shard_map.47.refs_4_.refs_0_), channel_id=1, source_target_pairs={{0,24},{4,28},{8,16},{12,20},{16,8},{20,12},{24,0},{28,4},{1,25},{... | collective-permute-start | bytes 294920 | tf_op jit(solution)/shard_map/ppermute | solution.py:260
  13.7 0.0 collective-permute-done.refs_1_
  13.7 0.5 %collective-permute-start.6 = (bf16[384,128]{1,0:T(8,128)(2,1)S(1)}, bf16[384,128]{1,0:T(8,128)(2,1)S(1)}, u32[]{:S(2)}, u32[]{:S(2)}) collective-permute-start(bf16[384,128]{1,0:T(8,128)(2,1)S(1)} %shard_map.47.refs_4_.refs_0_), channel_id=1, source_target_pairs={{0,16},{4,20},{8,24},{12,28},{16,0},{20,4},{24,8},{28,12},{1,17},{... | collective-permute-start | bytes 294920 | tf_op jit(solution)/shard_map/ppermute | solution.py:260
  14.2 0.0 collective-permute-done.1.refs_2_
  14.2 0.0 collective-permute-start.7
  14.2 0.8 %collective-permute-done.2.refs_3_ = bf16[384,128]{1,0:T(8,128)(2,1)S(1)} collective-permute-done((bf16[384,128]{1,0:T(8,128)(2,1)S(1)}, bf16[384,128]{1,0:T(8,128)(2,1)S(1)}, u32[]{:S(2)}, u32[]{:S(2)}) %collective-permute-start.2) | collective-permute-done | bytes 98336 | tf_op jit(solution)/shard_map/ppermute | solution.py:251
  15.0 0.0 collective-permute-done.4.refs_5_.refs_1_
  15.0 0.0 collective-permute-start.8
  15.0 2.3 %collective-permute-done.5.refs_6_.refs_2_ = bf16[384,128]{1,0:T(8,128)(2,1)S(1)} collective-permute-done((bf16[384,128]{1,0:T(8,128)(2,1)S(1)}, bf16[384,128]{1,0:T(8,128)(2,1)S(1)}, u32[]{:S(2)}, u32[]{:S(2)}) %collective-permute-start.5) | collective-permute-done | bytes 98336 | tf_op jit(solution)/shard_map/ppermute | solution.py:260
  17.3 0.0 collective-permute-start.9
  17.3 1.0 %collective-permute-done.6.refs_7_.refs_3_ = bf16[384,128]{1,0:T(8,128)(2,1)S(1)} collective-permute-done((bf16[384,128]{1,0:T(8,128)(2,1)S(1)}, bf16[384,128]{1,0:T(8,128)(2,1)S(1)}, u32[]{:S(2)}, u32[]{:S(2)}) %collective-permute-start.6) | collective-permute-done | bytes 98336 | tf_op jit(solution)/shard_map/ppermute | solution.py:260
  18.4 0.0 collective-permute-start.10
  18.4 0.6 %shard_map.48.mixed = bf16[4,128,384]{2,1,0:T(8,128)(2,1)S(1)} custom-call(f32[8,8,128]{2,1,0:T(8,128)S(1)} %get-tuple-element.12.table, bf16[384,128]{1,0:T(8,128)(2,1)S(1)} %get-tuple-element.13.refs_0_, bf16[384,128]{1,0:T(8,128)(2,1)S(1)} %collective-permute-done.refs_1_, bf16[384,128]{1,0:T(8,128)(2,1)S(1)} %collective-permute-done.1.refs_2_, ...), custom_call_target="tpu_custom_call" | custom-call | bytes 1212416 | tf_op jit(solution)/shard_map/pallas_call | solution.py:190
  18.9 0.0 collective-permute-done.7.refs_4_
  19.0 0.0 collective-permute-done.8.refs_5_
  19.0 0.0 collective-permute-done.9.refs_6_
  19.0 0.7 %collective-permute-done.10.refs_7_ = bf16[384,128]{1,0:T(8,128)(2,1)S(1)} collective-permute-done((bf16[384,128]{1,0:T(8,128)(2,1)S(1)}, bf16[384,128]{1,0:T(8,128)(2,1)S(1)}, u32[]{:S(2)}, u32[]{:S(2)}) %collective-permute-start.10) | collective-permute-done | bytes 98336 | tf_op jit(solution)/shard_map/ppermute | solution.py:265
  19.7 0.9 %shard_map.49 = f32[128,256]{1,0:T(8,128)} custom-call(bf16[4,128,384]{2,1,0:T(8,128)(2,1)S(1)} %shard_map.48.mixed, bf16[384,128]{1,0:T(8,128)(2,1)S(1)} %shard_map.47.refs_4_.refs_0_, bf16[384,128]{1,0:T(8,128)(2,1)S(1)} %collective-permute-done.4.refs_5_.refs_1_, bf16[384,128]{1,0:T(8,128)(2,1)S(1)} %collective-permute-done.5.refs_6_.refs_2_, ...), custom_call_target="tpu_custom_call" | custom-call | bytes 1310720 | tf_op jit(solution)/shard_map/pallas_call | solution.py:190
Async XLA Ops:
  0.0 9.1 %collective-permute-start.3 = (bf16[384,128]{1,0:T(8,128)(2,1)}, bf16[384,128]{1,0:T(8,128)(2,1)S(1)}, u32[]{:S(2)}, u32[]{:S(2)}) collective-permute-start(bf16[384,128]{1,0:T(8,128)(2,1)} %bitcast.1), channel_id=1, source_target_pairs={{0,8},{1,0},{2,16},{3,24},{4,12},{5,4},{6,20},{7,28},{8,25},{9,1},... | collective-permute-start | bytes 294920 | tf_op jit(solution)/shard_map/ppermute | solution.py:221
  4.3 9.5 %collective-permute-start = (bf16[384,128]{1,0:T(8,128)(2,1)S(1)}, bf16[384,128]{1,0:T(8,128)(2,1)S(1)}, u32[]{:S(2)}, u32[]{:S(2)}) collective-permute-start(bf16[384,128]{1,0:T(8,128)(2,1)S(1)} %get-tuple-element.13.refs_0_), channel_id=1, source_target_pairs={{0,1},{1,9},{2,3},{3,2},{4,5},{5,13},{6,7},{7,6},{8,0},{9,8},{10,1... | collective-permute-start | bytes 294920 | tf_op jit(solution)/shard_map/ppermute | solution.py:251
  4.4 9.8 %collective-permute-start.1 = (bf16[384,128]{1,0:T(8,128)(2,1)S(1)}, bf16[384,128]{1,0:T(8,128)(2,1)S(1)}, u32[]{:S(2)}, u32[]{:S(2)}) collective-permute-start(bf16[384,128]{1,0:T(8,128)(2,1)S(1)} %get-tuple-element.13.refs_0_), channel_id=1, source_target_pairs={{0,3},{1,2},{2,1},{3,27},{4,7},{5,6},{6,5},{7,31},{8,11},{9,10},{1... | collective-permute-start | bytes 294920 | tf_op jit(solution)/shard_map/ppermute | solution.py:251
  8.6 6.4 %collective-permute-start.2 = (bf16[384,128]{1,0:T(8,128)(2,1)S(1)}, bf16[384,128]{1,0:T(8,128)(2,1)S(1)}, u32[]{:S(2)}, u32[]{:S(2)}) collective-permute-start(bf16[384,128]{1,0:T(8,128)(2,1)S(1)} %get-tuple-element.13.refs_0_), channel_id=1, source_target_pairs={{0,2},{1,3},{2,18},{3,1},{4,6},{5,7},{6,22},{7,5},{8,10},{9,11},{1... | collective-permute-start | bytes 294920 | tf_op jit(solution)/shard_map/ppermute | solution.py:251
  9.4 5.6 %collective-permute-start.4 = (bf16[384,128]{1,0:T(8,128)(2,1)S(1)}, bf16[384,128]{1,0:T(8,128)(2,1)S(1)}, u32[]{:S(2)}, u32[]{:S(2)}) collective-permute-start(bf16[384,128]{1,0:T(8,128)(2,1)S(1)} %shard_map.47.refs_4_.refs_0_), channel_id=1, source_target_pairs={{0,8},{4,12},{8,0},{12,4},{16,24},{20,28},{24,16},{28,20},{1,9},{5... | collective-permute-start | bytes 294920 | tf_op jit(solution)/shard_map/ppermute | solution.py:260
  10.8 6.5 %collective-permute-start.5 = (bf16[384,128]{1,0:T(8,128)(2,1)S(1)}, bf16[384,128]{1,0:T(8,128)(2,1)S(1)}, u32[]{:S(2)}, u32[]{:S(2)}) collective-permute-start(bf16[384,128]{1,0:T(8,128)(2,1)S(1)} %shard_map.47.refs_4_.refs_0_), channel_id=1, source_target_pairs={{0,24},{4,28},{8,16},{12,20},{16,8},{20,12},{24,0},{28,4},{1,25},{... | collective-permute-start | bytes 294920 | tf_op jit(solution)/shard_map/ppermute | solution.py:260
  13.7 4.6 %collective-permute-start.6 = (bf16[384,128]{1,0:T(8,128)(2,1)S(1)}, bf16[384,128]{1,0:T(8,128)(2,1)S(1)}, u32[]{:S(2)}, u32[]{:S(2)}) collective-permute-start(bf16[384,128]{1,0:T(8,128)(2,1)S(1)} %shard_map.47.refs_4_.refs_0_), channel_id=1, source_target_pairs={{0,16},{4,20},{8,24},{12,28},{16,0},{20,4},{24,8},{28,12},{1,17},{... | collective-permute-start | bytes 294920 | tf_op jit(solution)/shard_map/ppermute | solution.py:260
  14.2 4.7 %collective-permute-start.7 = (bf16[384,128]{1,0:T(8,128)(2,1)S(1)}, bf16[384,128]{1,0:T(8,128)(2,1)S(1)}, u32[]{:S(2)}, u32[]{:S(2)}) collective-permute-start(bf16[384,128]{1,0:T(8,128)(2,1)S(1)} %shard_map.47.refs_4_.refs_0_), channel_id=1, source_target_pairs={{0,4},{4,0},{8,12},{12,8},{16,20},{20,16},{24,28},{28,24},{1,5},{5... | collective-permute-start | bytes 294920 | tf_op jit(solution)/shard_map/ppermute | solution.py:265
  15.0 4.0 %collective-permute-start.8 = (bf16[384,128]{1,0:T(8,128)(2,1)S(1)}, bf16[384,128]{1,0:T(8,128)(2,1)S(1)}, u32[]{:S(2)}, u32[]{:S(2)}) collective-permute-start(bf16[384,128]{1,0:T(8,128)(2,1)S(1)} %collective-permute-done.4.refs_5_.refs_1_), channel_id=1, source_target_pairs={{0,4},{4,0},{8,12},{12,8},{16,20},{20,16},{24,28},{28,24},{1,5},{5... | collective-permute-start | bytes 294920 | tf_op jit(solution)/shard_map/ppermute | solution.py:265
  17.3 1.7 %collective-permute-start.9 = (bf16[384,128]{1,0:T(8,128)(2,1)S(1)}, bf16[384,128]{1,0:T(8,128)(2,1)S(1)}, u32[]{:S(2)}, u32[]{:S(2)}) collective-permute-start(bf16[384,128]{1,0:T(8,128)(2,1)S(1)} %collective-permute-done.5.refs_6_.refs_2_), channel_id=1, source_target_pairs={{0,4},{4,0},{8,12},{12,8},{16,20},{20,16},{24,28},{28,24},{1,5},{5... | collective-permute-start | bytes 294920 | tf_op jit(solution)/shard_map/ppermute | solution.py:265
  18.4 1.3 %collective-permute-start.10 = (bf16[384,128]{1,0:T(8,128)(2,1)S(1)}, bf16[384,128]{1,0:T(8,128)(2,1)S(1)}, u32[]{:S(2)}, u32[]{:S(2)}) collective-permute-start(bf16[384,128]{1,0:T(8,128)(2,1)S(1)} %collective-permute-done.6.refs_7_.refs_3_), channel_id=1, source_target_pairs={{0,4},{4,0},{8,12},{12,8},{16,20},{20,16},{24,28},{28,24},{1,5},{5... | collective-permute-start | bytes 294920 | tf_op jit(solution)/shard_map/ppermute | solution.py:265

commit v5 on v4

--- a/solution.py
+++ b/solution.py
@@ -172,18 +172,23 @@
 
 
 def gram_kernel(planes, mixed, *refs):
-    mine, theirs, out = refs[:planes], refs[planes : 2 * planes], refs[2 * planes]
-    total = None
-    for away in range(planes):
-        both = jnp.concatenate([mine[away][...], theirs[away][...]], axis=1)
-        part = jnp.dot(mixed[away], both, preferred_element_type=jnp.float32)
-        total = part if total is None else total + part
+    mine, theirs, (out, halves, arrivals) = refs[:planes], refs[planes : 2 * planes], refs[2 * planes :]
     core = lax.axis_index("dp") & 1
-    out[:, pl.ds(pl.multiple_of(core * LANES, LANES), LANES)] = total[:, :LANES]
-    out[:, pl.ds(pl.multiple_of((1 - core) * LANES, LANES), LANES)] = total[:, LANES:]
-
-
-def call(kernel, out_shape, operands, in_specs, scratch=(), flops=0):
+    copies = []
+    for half, (blocks, place) in enumerate(((mine, core), (theirs, 1 - core))):
+        total = None
+        for away in range(planes):
+            part = jnp.dot(mixed[away], blocks[away][...], preferred_element_type=jnp.float32)
+            total = part if total is None else total + part
+        halves[half] = total
+        columns = pl.ds(pl.multiple_of(place * LANES, LANES), LANES)
+        copies.append(pltpu.make_async_copy(halves.at[half], out.at[:, columns], arrivals.at[half]))
+        copies[half].start()
+    for copy in copies:
+        copy.wait()
+
+
+def call(kernel, out_shape, operands, in_specs, scratch=(), flops=0, out_spec=VMEM):
     sizes = jax.tree.leaves(out_shape) + list(operands)
     held = sum(item.size * item.dtype.itemsize for item in sizes)
     spare = sum(4 * math.prod(item.shape) for item in scratch if item.memory_space == pltpu.VMEM)
@@ -191,7 +196,7 @@
         kernel,
         out_shape=out_shape,
         in_specs=in_specs,
-        out_specs=jax.tree.map(lambda _: VMEM, out_shape),
+        out_specs=jax.tree.map(lambda _: out_spec, out_shape),
         scratch_shapes=list(scratch),
         compiler_params=pltpu.CompilerParams(vmem_limit_bytes=(6 << 20) + 2 * held + spare),
         cost_estimate=pl.CostEstimate(flops=flops, bytes_accessed=held, transcendentals=0),
@@ -278,6 +283,8 @@
         jax.ShapeDtypeStruct((rows, CORES * rows), jnp.float32),
         (mixed, *mine, *theirs),
         [VMEM] * (1 + 2 * planes),
+        [pltpu.VMEM((CORES, rows, LANES), jnp.float32), pltpu.SemaphoreType.DMA((CORES,))],
+        out_spec=pl.BlockSpec(memory_space=pl.ANY),
     )
 
 

time: 20.8 us -> 20.8 us (level)
  transfers between devices with their start and end apart: 11 -> 11, of which waited for: 4 -> 4; matrix products, arithmetic and copies ran while one was open for 0% -> 0% of each run, Pallas kernels for 11% -> 10%
where the time goes in v5:
time: 20.8 us; the launch traced here: 20.7 us
  starting transfers between devices  12.6 us (61%)
  waiting for transfers between devices  4.83 us (23%)
  Pallas kernels  3.17 us (15%)
    ppermute x3, starting transfers between devices, shards(): lax.ppermute(mixed_arrived, 'dp', [(i, i ^ away * CORES) for i in range(s...  4.84 us
    ppermute x3, starting transfers between devices, shards(): along.append(lax.ppermute(smooth, ('dp', 'pencil'), pairs))  4.83 us
    ppermute x3, waiting for transfers between devices, shards(): lax.ppermute(mixed_arrived, 'dp', [(i, i ^ away * CORES) for i in range(s...  3.37 us
    pallas_call x4, Pallas kernels, call(): pl.pallas_call(kernel, out_shape=out_shape, in_specs=in_specs, out_specs=...  3.17 us
    ppermute x1, starting transfers between devices, shards(): arrived = lax.ppermute(field, ('dp', 'pencil'), route)  2.94 us
    ppermute x3, waiting for transfers between devices, shards(): along.append(lax.ppermute(smooth, ('dp', 'pencil'), pairs))  0.76 us
    ppermute x4, waiting for transfers between devices, shards(): theirs.append(lax.ppermute(item, 'dp', [(i, i ^ 1) for i in range(spread)]))  0.7 us
  transfers between devices with their start and end apart: 11, of which 4 were waited for; matrix products, arithmetic and copies ran while one was open for 0% of the time, Pallas kernels for 10%

profile of v5, /device:TPU:0, one launch (start us, length us, event | category | flops | bytes accessed | tf_op | source)
XLA Modules:
  0.0 20.7 jit_solution(5446850571589590303)
XLA Ops:
  0.0 2.9 %collective-permute-start.3 = (bf16[384,128]{1,0:T(8,128)(2,1)}, bf16[384,128]{1,0:T(8,128)(2,1)S(1)}, u32[]{:S(2)}, u32[]{:S(2)}) collective-permute-start(bf16[384,128]{1,0:T(8,128)(2,1)} %bitcast.1), channel_id=1, source_target_pairs={{0,8},{1,0},{2,16},{3,24},{4,12},{5,4},{6,20},{7,28},{8,25},{9,1},... | collective-permute-start | bytes 294920 | tf_op jit(solution)/shard_map/ppermute | solution.py:226
  2.9 1.3 %shard_map.46 = (bf16[384,128]{1,0:T(8,128)(2,1)S(1)}, bf16[192,192]{1,0:T(8,128)(2,1)S(1)}, f32[8,8,128]{2,1,0:T(8,128)S(1)}, f32[8,8,128]{2,1,0:T(8,128)S(1)}) custom-call(s32[3,3]{1,0:T(4,128)} %refs_0_.1, s32[3,3,4]{2,1,0:T(4,128)} %refs_1_.1, f32[3,3]{1,0:T(4,128)} %refs_2_.1, bf16[384,128]{1,0:T(8,128)(2,1)} %bitcast.2), custom_call_target="tpu_custom_call" | custom-call | bytes 336088 | tf_op jit(solution)/shard_map/pallas_call | solution.py:195
  4.3 0.1 collective-permute-start
  4.4 4.2 %collective-permute-start.1 = (bf16[384,128]{1,0:T(8,128)(2,1)S(1)}, bf16[384,128]{1,0:T(8,128)(2,1)S(1)}, u32[]{:S(2)}, u32[]{:S(2)}) collective-permute-start(bf16[384,128]{1,0:T(8,128)(2,1)S(1)} %get-tuple-element.13.refs_0_), channel_id=1, source_target_pairs={{0,3},{1,2},{2,1},{3,27},{4,7},{5,6},{6,5},{7,31},{8,11},{9,10},{1... | collective-permute-start | bytes 294920 | tf_op jit(solution)/shard_map/ppermute | solution.py:256
  8.6 0.5 %collective-permute-start.2 = (bf16[384,128]{1,0:T(8,128)(2,1)S(1)}, bf16[384,128]{1,0:T(8,128)(2,1)S(1)}, u32[]{:S(2)}, u32[]{:S(2)}) collective-permute-start(bf16[384,128]{1,0:T(8,128)(2,1)S(1)} %get-tuple-element.13.refs_0_), channel_id=1, source_target_pairs={{0,2},{1,3},{2,18},{3,1},{4,6},{5,7},{6,22},{7,5},{8,10},{9,11},{1... | collective-permute-start | bytes 294920 | tf_op jit(solution)/shard_map/ppermute | solution.py:256
  9.1 0.0 collective-permute-done.3.field
  9.1 0.3 %shard_map.47.refs_4_.refs_0_ = bf16[384,128]{1,0:T(8,128)(2,1)S(1)} custom-call(bf16[384,128]{1,0:T(8,128)(2,1)S(1)} %collective-permute-done.3.field, bf16[192,192]{1,0:T(8,128)(2,1)S(1)} %get-tuple-element.14.blocks_z, f32[8,8,128]{2,1,0:T(8,128)S(1)} %get-tuple-element.15.table_x), custom_call_target="tpu_custom_call" | custom-call | bytes 303104 | tf_op jit(solution)/shard_map/pallas_call | solution.py:195
  9.4 1.4 %collective-permute-start.4 = (bf16[384,128]{1,0:T(8,128)(2,1)S(1)}, bf16[384,128]{1,0:T(8,128)(2,1)S(1)}, u32[]{:S(2)}, u32[]{:S(2)}) collective-permute-start(bf16[384,128]{1,0:T(8,128)(2,1)S(1)} %shard_map.47.refs_4_.refs_0_), channel_id=1, source_target_pairs={{0,8},{4,12},{8,0},{12,4},{16,24},{20,28},{24,16},{28,20},{1,9},{5... | collective-permute-start | bytes 294920 | tf_op jit(solution)/shard_map/ppermute | solution.py:265
  10.8 3.0 %collective-permute-start.5 = (bf16[384,128]{1,0:T(8,128)(2,1)S(1)}, bf16[384,128]{1,0:T(8,128)(2,1)S(1)}, u32[]{:S(2)}, u32[]{:S(2)}) collective-permute-start(bf16[384,128]{1,0:T(8,128)(2,1)S(1)} %shard_map.47.refs_4_.refs_0_), channel_id=1, source_target_pairs={{0,24},{4,28},{8,16},{12,20},{16,8},{20,12},{24,0},{28,4},{1,25},{... | collective-permute-start | bytes 294920 | tf_op jit(solution)/shard_map/ppermute | solution.py:265
  13.7 0.0 collective-permute-done.refs_1_
  13.7 0.5 %collective-permute-start.6 = (bf16[384,128]{1,0:T(8,128)(2,1)S(1)}, bf16[384,128]{1,0:T(8,128)(2,1)S(1)}, u32[]{:S(2)}, u32[]{:S(2)}) collective-permute-start(bf16[384,128]{1,0:T(8,128)(2,1)S(1)} %shard_map.47.refs_4_.refs_0_), channel_id=1, source_target_pairs={{0,16},{4,20},{8,24},{12,28},{16,0},{20,4},{24,8},{28,12},{1,17},{... | collective-permute-start | bytes 294920 | tf_op jit(solution)/shard_map/ppermute | solution.py:265
  14.2 0.0 collective-permute-done.1.refs_2_
  14.2 0.0 collective-permute-start.7
  14.2 0.8 %collective-permute-done.2.refs_3_ = bf16[384,128]{1,0:T(8,128)(2,1)S(1)} collective-permute-done((bf16[384,128]{1,0:T(8,128)(2,1)S(1)}, bf16[384,128]{1,0:T(8,128)(2,1)S(1)}, u32[]{:S(2)}, u32[]{:S(2)}) %collective-permute-start.2) | collective-permute-done | bytes 98336 | tf_op jit(solution)/shard_map/ppermute | solution.py:256
  15.0 0.0 collective-permute-done.4.refs_5_.refs_1_
  15.0 0.0 collective-permute-start.8
  15.0 2.3 %collective-permute-done.5.refs_6_.refs_2_ = bf16[384,128]{1,0:T(8,128)(2,1)S(1)} collective-permute-done((bf16[384,128]{1,0:T(8,128)(2,1)S(1)}, bf16[384,128]{1,0:T(8,128)(2,1)S(1)}, u32[]{:S(2)}, u32[]{:S(2)}) %collective-permute-start.5) | collective-permute-done | bytes 98336 | tf_op jit(solution)/shard_map/ppermute | solution.py:265
  17.3 0.0 collective-permute-start.9
  17.3 1.0 %collective-permute-done.6.refs_7_.refs_3_ = bf16[384,128]{1,0:T(8,128)(2,1)S(1)} collective-permute-done((bf16[384,128]{1,0:T(8,128)(2,1)S(1)}, bf16[384,128]{1,0:T(8,128)(2,1)S(1)}, u32[]{:S(2)}, u32[]{:S(2)}) %collective-permute-start.6) | collective-permute-done | bytes 98336 | tf_op jit(solution)/shard_map/ppermute | solution.py:265
  18.4 0.0 collective-permute-start.10
  18.4 0.6 %shard_map.48.mixed = bf16[4,128,384]{2,1,0:T(8,128)(2,1)S(1)} custom-call(f32[8,8,128]{2,1,0:T(8,128)S(1)} %get-tuple-element.12.table, bf16[384,128]{1,0:T(8,128)(2,1)S(1)} %get-tuple-element.13.refs_0_, bf16[384,128]{1,0:T(8,128)(2,1)S(1)} %collective-permute-done.refs_1_, bf16[384,128]{1,0:T(8,128)(2,1)S(1)} %collective-permute-done.1.refs_2_, ...), custom_call_target="tpu_custom_call" | custom-call | bytes 1212416 | tf_op jit(solution)/shard_map/pallas_call | solution.py:195
  18.9 0.0 collective-permute-done.7.refs_4_
  19.0 0.0 collective-permute-done.8.refs_5_
  19.0 0.0 collective-permute-done.9.refs_6_
  19.0 0.7 %collective-permute-done.10.refs_7_ = bf16[384,128]{1,0:T(8,128)(2,1)S(1)} collective-permute-done((bf16[384,128]{1,0:T(8,128)(2,1)S(1)}, bf16[384,128]{1,0:T(8,128)(2,1)S(1)}, u32[]{:S(2)}, u32[]{:S(2)}) %collective-permute-start.10) | collective-permute-done | bytes 98336 | tf_op jit(solution)/shard_map/ppermute | solution.py:270
  19.7 1.0 %shard_map.49 = f32[128,256]{1,0:T(8,128)} custom-call(bf16[4,128,384]{2,1,0:T(8,128)(2,1)S(1)} %shard_map.48.mixed, bf16[384,128]{1,0:T(8,128)(2,1)S(1)} %shard_map.47.refs_4_.refs_0_, bf16[384,128]{1,0:T(8,128)(2,1)S(1)} %collective-permute-done.4.refs_5_.refs_1_, bf16[384,128]{1,0:T(8,128)(2,1)S(1)} %collective-permute-done.5.refs_6_.refs_2_, ...), custom_call_target="tpu_custom_call" | custom-call | bytes 1310720 | tf_op jit(solution)/shard_map/pallas_call | solution.py:195
Async XLA Ops:
  0.0 9.1 %collective-permute-start.3 = (bf16[384,128]{1,0:T(8,128)(2,1)}, bf16[384,128]{1,0:T(8,128)(2,1)S(1)}, u32[]{:S(2)}, u32[]{:S(2)}) collective-permute-start(bf16[384,128]{1,0:T(8,128)(2,1)} %bitcast.1), channel_id=1, source_target_pairs={{0,8},{1,0},{2,16},{3,24},{4,12},{5,4},{6,20},{7,28},{8,25},{9,1},... | collective-permute-start | bytes 294920 | tf_op jit(solution)/shard_map/ppermute | solution.py:226
  4.3 9.5 %collective-permute-start = (bf16[384,128]{1,0:T(8,128)(2,1)S(1)}, bf16[384,128]{1,0:T(8,128)(2,1)S(1)}, u32[]{:S(2)}, u32[]{:S(2)}) collective-permute-start(bf16[384,128]{1,0:T(8,128)(2,1)S(1)} %get-tuple-element.13.refs_0_), channel_id=1, source_target_pairs={{0,1},{1,9},{2,3},{3,2},{4,5},{5,13},{6,7},{7,6},{8,0},{9,8},{10,1... | collective-permute-start | bytes 294920 | tf_op jit(solution)/shard_map/ppermute | solution.py:256
  4.4 9.8 %collective-permute-start.1 = (bf16[384,128]{1,0:T(8,128)(2,1)S(1)}, bf16[384,128]{1,0:T(8,128)(2,1)S(1)}, u32[]{:S(2)}, u32[]{:S(2)}) collective-permute-start(bf16[384,128]{1,0:T(8,128)(2,1)S(1)} %get-tuple-element.13.refs_0_), channel_id=1, source_target_pairs={{0,3},{1,2},{2,1},{3,27},{4,7},{5,6},{6,5},{7,31},{8,11},{9,10},{1... | collective-permute-start | bytes 294920 | tf_op jit(solution)/shard_map/ppermute | solution.py:256
  8.6 6.4 %collective-permute-start.2 = (bf16[384,128]{1,0:T(8,128)(2,1)S(1)}, bf16[384,128]{1,0:T(8,128)(2,1)S(1)}, u32[]{:S(2)}, u32[]{:S(2)}) collective-permute-start(bf16[384,128]{1,0:T(8,128)(2,1)S(1)} %get-tuple-element.13.refs_0_), channel_id=1, source_target_pairs={{0,2},{1,3},{2,18},{3,1},{4,6},{5,7},{6,22},{7,5},{8,10},{9,11},{1... | collective-permute-start | bytes 294920 | tf_op jit(solution)/shard_map/ppermute | solution.py:256
  9.4 5.6 %collective-permute-start.4 = (bf16[384,128]{1,0:T(8,128)(2,1)S(1)}, bf16[384,128]{1,0:T(8,128)(2,1)S(1)}, u32[]{:S(2)}, u32[]{:S(2)}) collective-permute-start(bf16[384,128]{1,0:T(8,128)(2,1)S(1)} %shard_map.47.refs_4_.refs_0_), channel_id=1, source_target_pairs={{0,8},{4,12},{8,0},{12,4},{16,24},{20,28},{24,16},{28,20},{1,9},{5... | collective-permute-start | bytes 294920 | tf_op jit(solution)/shard_map/ppermute | solution.py:265
  10.8 6.5 %collective-permute-start.5 = (bf16[384,128]{1,0:T(8,128)(2,1)S(1)}, bf16[384,128]{1,0:T(8,128)(2,1)S(1)}, u32[]{:S(2)}, u32[]{:S(2)}) collective-permute-start(bf16[384,128]{1,0:T(8,128)(2,1)S(1)} %shard_map.47.refs_4_.refs_0_), channel_id=1, source_target_pairs={{0,24},{4,28},{8,16},{12,20},{16,8},{20,12},{24,0},{28,4},{1,25},{... | collective-permute-start | bytes 294920 | tf_op jit(solution)/shard_map/ppermute | solution.py:265
  13.7 4.6 %collective-permute-start.6 = (bf16[384,128]{1,0:T(8,128)(2,1)S(1)}, bf16[384,128]{1,0:T(8,128)(2,1)S(1)}, u32[]{:S(2)}, u32[]{:S(2)}) collective-permute-start(bf16[384,128]{1,0:T(8,128)(2,1)S(1)} %shard_map.47.refs_4_.refs_0_), channel_id=1, source_target_pairs={{0,16},{4,20},{8,24},{12,28},{16,0},{20,4},{24,8},{28,12},{1,17},{... | collective-permute-start | bytes 294920 | tf_op jit(solution)/shard_map/ppermute | solution.py:265
  14.2 4.7 %collective-permute-start.7 = (bf16[384,128]{1,0:T(8,128)(2,1)S(1)}, bf16[384,128]{1,0:T(8,128)(2,1)S(1)}, u32[]{:S(2)}, u32[]{:S(2)}) collective-permute-start(bf16[384,128]{1,0:T(8,128)(2,1)S(1)} %shard_map.47.refs_4_.refs_0_), channel_id=1, source_target_pairs={{0,4},{4,0},{8,12},{12,8},{16,20},{20,16},{24,28},{28,24},{1,5},{5... | collective-permute-start | bytes 294920 | tf_op jit(solution)/shard_map/ppermute | solution.py:270
  15.0 4.0 %collective-permute-start.8 = (bf16[384,128]{1,0:T(8,128)(2,1)S(1)}, bf16[384,128]{1,0:T(8,128)(2,1)S(1)}, u32[]{:S(2)}, u32[]{:S(2)}) collective-permute-start(bf16[384,128]{1,0:T(8,128)(2,1)S(1)} %collective-permute-done.4.refs_5_.refs_1_), channel_id=1, source_target_pairs={{0,4},{4,0},{8,12},{12,8},{16,20},{20,16},{24,28},{28,24},{1,5},{5... | collective-permute-start | bytes 294920 | tf_op jit(solution)/shard_map/ppermute | solution.py:270
  17.3 1.7 %collective-permute-start.9 = (bf16[384,128]{1,0:T(8,128)(2,1)S(1)}, bf16[384,128]{1,0:T(8,128)(2,1)S(1)}, u32[]{:S(2)}, u32[]{:S(2)}) collective-permute-start(bf16[384,128]{1,0:T(8,128)(2,1)S(1)} %collective-permute-done.5.refs_6_.refs_2_), channel_id=1, source_target_pairs={{0,4},{4,0},{8,12},{12,8},{16,20},{20,16},{24,28},{28,24},{1,5},{5... | collective-permute-start | bytes 294920 | tf_op jit(solution)/shard_map/ppermute | solution.py:270
  18.4 1.3 %collective-permute-start.10 = (bf16[384,128]{1,0:T(8,128)(2,1)S(1)}, bf16[384,128]{1,0:T(8,128)(2,1)S(1)}, u32[]{:S(2)}, u32[]{:S(2)}) collective-permute-start(bf16[384,128]{1,0:T(8,128)(2,1)S(1)} %collective-permute-done.6.refs_7_.refs_3_), channel_id=1, source_target_pairs={{0,4},{4,0},{8,12},{12,8},{16,20},{20,16},{24,28},{28,24},{1,5},{5... | collective-permute-start | bytes 294920 | tf_op jit(solution)/shard_map/ppermute | solution.py:270
